TPU v7x, 128 devices: a whole 4x4x4 slice. The times are simulated.
128 devices in a mesh: cell: 16 (over z, x), level: 4 (over y), rep: 2 (over core).
Axes of the slice: x: 4, y: 4, z: 4, core: 2. Of those that a mesh axis runs over, the one named last changes fastest.
Arguments:
- resident_pos: float32 [2, 32, 128, 2048], P(None, 'rep', 'level', 'cell'), may hold values from -0.5 to 0.5
- resident_strength: float32 [32, 128, 2048], P('rep', 'level', 'cell'), may hold values from -0.51 to 0.51
- mover_pos: float32 [2, 2, 4, 65536], P(None, 'rep', 'level', 'cell'), may hold values from -0.5 to 0.5
- mover_strength: float32 [2, 4, 65536], P('rep', 'level', 'cell'), may hold values from -0.51 to 0.51
- mover_owner: int32 [2, 4, 65536], P('rep', 'level', 'cell'), may hold values from 0 to 15, as said below
- mover_leaf: int32 [2, 4, 65536], P('rep', 'level', 'cell'), may hold values from 0 to 4095, as said below
- mover_slot: int32 [2, 4, 65536], P('rep', 'level', 'cell'), may hold values from 0 to 15
Outputs:
- velocity: float32 [2, 32, 128, 2048], P(None, 'rep', 'level', 'cell')
Inputs may be any that keep to these rules, and one draw needn't show every extreme that they name: `mover_owner`: for one rep and level index, the 4096 movers of one device name one owner at most 1024 times, and one owner is named exactly 1024 times by every device. `mover_leaf`: leaf key y * 128 + x inside the owner's domain; for one rep and level index no (owner, leaf, slot) triple appears twice.
All inputs are finite; a program needn't handle non-finite values.
Results may differ from a plain program's by a relative error of at most 0.0003.
Values sent between devices are 32-bit elements; how exact they have to be, the bound alone decides.
No kernel may reach another device: no remote copies, remote signals or barrier semaphores. Data moves between devices by JAX's collectives and lax.ppermute only.
A program may use at most 192 MiB of HBM per device.

v0:
```python
import math

import jax
import jax.numpy as jnp
import numpy as np
from jax import lax
from jax.sharding import PartitionSpec as P

ORDER = 10
HALO_LEVELS = 4
CAP = 1024


precise = lax.Precision.HIGHEST
blob_square = 0.09


def with_halo(shard, sides, width):
    for axis, dim in sides:
        devices, length = (lax.axis_size(axis), shard.shape[dim])
        up = [(i, (i + 1) % devices) for i in range(devices - 1)]
        down = [(j, i) for i, j in up]
        last = lax.slice_in_dim(shard, length - width, length, axis=dim)
        first = lax.slice_in_dim(shard, 0, width, axis=dim)
        before = lax.ppermute(last, axis, up)
        after = lax.ppermute(first, axis, down)
        shard = jnp.concatenate([before, shard, after], axis=dim)
    return shard


def real_form(matrix):
    top_rows = np.concatenate([matrix.real, -matrix.imag], axis=1)
    low_rows = np.concatenate([matrix.imag, matrix.real], axis=1)
    return np.concatenate([top_rows, low_rows], axis=0)


def child_offset(parity_x, parity_y):
    return complex((parity_x - 0.5) / 2.0, (parity_y - 0.5) / 2.0)


def upward_table(parity_x, parity_y):
    offset = child_offset(parity_x, parity_y)
    matrix = np.zeros((ORDER, ORDER), complex)
    for k in range(ORDER):
        for m in range(k + 1):
            matrix[k, m] = math.comb(k, m) * 0.5**m * offset ** (k - m)
    return real_form(matrix)


def downward_table(parity_x, parity_y):
    offset = child_offset(parity_x, parity_y)
    matrix = np.zeros((ORDER, ORDER), complex)
    for m in range(ORDER):
        for l in range(m, ORDER):
            matrix[m, l] = 0.5 ** (m + 1) * math.comb(l, m) * offset ** (l - m)
    return real_form(matrix)


def far_table(step_x, step_y):
    distance = complex(step_x, step_y)
    matrix = np.zeros((ORDER, ORDER), complex)
    for l in range(ORDER):
        for k in range(ORDER):
            matrix[l, k] = (-1) ** (k + 1) * math.comb(k + l, l) * distance ** (-(k + l + 1))
    return real_form(matrix)


def apply_matrix(matrix, level_field):
    return jnp.einsum(
        "ij,jyx->iyx", jnp.asarray(matrix, dtype=jnp.float32), level_field, precision=precise
    )


def upward(level_field):
    summed = None
    for parity_y in (0, 1):
        for parity_x in (0, 1):
            product = apply_matrix(
                upward_table(parity_x, parity_y), level_field[:, parity_y::2, parity_x::2]
            )
            summed = product if summed is None else summed + product
    return summed


def downward(parent):
    channels, cells_y, cells_x = parent.shape
    pieces = jnp.stack(
        [
            jnp.stack(
                [apply_matrix(downward_table(parity_x, parity_y), parent) for parity_x in (0, 1)]
            )
            for parity_y in (0, 1)
        ]
    )
    return pieces.transpose(2, 3, 0, 4, 1).reshape(channels, 2 * cells_y, 2 * cells_x)


def grouped_far(padded, margin_cells, cells_y, cells_x):
    classes = []
    for parity_y in (0, 1):
        row_parts = []
        for parity_x in (0, 1):
            pieces = []
            blocks = []
            for step_y in range(-2 - parity_y, 4 - parity_y):
                for step_x in range(-2 - parity_x, 4 - parity_x):
                    if max(abs(step_x), abs(step_y)) <= 1:
                        continue
                    first_y = margin_cells + parity_y + step_y
                    first_x = margin_cells + parity_x + step_x
                    pieces.append(
                        padded[:, first_y : first_y + cells_y : 2, first_x : first_x + cells_x : 2]
                    )
                    blocks.append(far_table(step_x, step_y))
            row_parts.append(
                apply_matrix(np.concatenate(blocks, axis=1), jnp.concatenate(pieces, axis=0))
            )
        classes.append(jnp.stack(row_parts))
    joined = jnp.stack(classes)
    return joined.transpose(2, 3, 0, 4, 1).reshape(joined.shape[2], cells_y, cells_x)


def top_far(level_field):
    channels, cells_y, cells_x = level_field.shape
    reach_y = cells_y - 1
    reach_x = cells_x - 1
    padded = jnp.pad(level_field, ((0, 0), (reach_y, reach_y), (reach_x, reach_x)))
    summed = jnp.zeros(level_field.shape, jnp.float32)
    for step_y in range(-reach_y, reach_y + 1):
        for step_x in range(-reach_x, reach_x + 1):
            if max(abs(step_x), abs(step_y)) <= 1:
                continue
            source = padded[
                :,
                reach_y + step_y : reach_y + step_y + cells_y,
                reach_x + step_x : reach_x + step_x + cells_x,
            ]
            summed = summed + apply_matrix(far_table(step_x, step_y), source)
    return summed


def moments(pos_x, pos_y, strength):
    real_power = jnp.ones_like(pos_x)
    imag_power = jnp.zeros_like(pos_x)
    real_rows = []
    imag_rows = []
    for k in range(ORDER):
        real_rows.append(jnp.sum(strength * real_power, axis=0))
        imag_rows.append(jnp.sum(strength * imag_power, axis=0))
        real_power, imag_power = (
            real_power * pos_x - imag_power * pos_y,
            real_power * pos_y + imag_power * pos_x,
        )
    return jnp.stack(real_rows + imag_rows)


def evaluate(local_field, pos_x, pos_y):
    real_acc = jnp.broadcast_to(local_field[ORDER - 1], pos_x.shape)
    imag_acc = jnp.broadcast_to(local_field[2 * ORDER - 1], pos_x.shape)
    for l in range(ORDER - 2, -1, -1):
        real_acc, imag_acc = (
            real_acc * pos_x - imag_acc * pos_y + local_field[l],
            real_acc * pos_y + imag_acc * pos_x + local_field[ORDER + l],
        )
    return (real_acc, imag_acc)


def framing(level_field):
    return with_halo(level_field, (("cell", 2), ("level", 1)), 3)


def local(
    resident_pos, resident_strength, mover_pos, mover_strength, mover_owner, mover_leaf, mover_slot
):
    cell_count = lax.axis_size("cell")
    level_count = lax.axis_size("level")
    half_slots, cells_y, cells_x = resident_strength.shape
    leaves = cells_y * cells_x
    owner_cell = mover_owner.reshape(-1)
    address = mover_slot.reshape(-1) * leaves + mover_leaf.reshape(-1)
    peer_ids = jnp.arange(cell_count, dtype=jnp.int32)
    onehot = (owner_cell[:, None] == peer_ids[None, :]).astype(jnp.int32)
    rank_in_owner = jnp.sum(jnp.cumsum(onehot, axis=0) * onehot, axis=1) - 1
    values = jnp.concatenate([mover_pos.reshape(2, -1), mover_strength.reshape(1, -1)])
    outgoing = (
        jnp.zeros((3, cell_count, CAP), jnp.float32).at[:, owner_cell, rank_in_owner].set(values)
    )
    addresses = (
        jnp.full((1, cell_count, CAP), half_slots * leaves, jnp.int32)
        .at[0, owner_cell, rank_in_owner]
        .set(address)
    )
    arrived, arrived_at = (
        lax.all_to_all(outgoing, "cell", split_axis=1, concat_axis=1, tiled=True),
        lax.all_to_all(addresses, "cell", split_axis=1, concat_axis=1, tiled=True),
    )
    resident = jnp.concatenate([resident_pos.reshape(2, -1), resident_strength.reshape(1, -1)])
    settled = resident.at[:, arrived_at.reshape(-1)].set(arrived.reshape(3, -1), mode="drop")
    particles = settled.reshape(3, half_slots, cells_y, cells_x)
    whole = lax.all_gather(particles, "rep", axis=1, tiled=True)
    framed = with_halo(whole, (("cell", 3), ("level", 2)), 1)
    whole_inner = framed[:, :, 1:-1, 1:-1]
    level_zero = moments(whole_inner[0], whole_inner[1], whole_inner[2])
    owned = [level_zero]
    for k in range(HALO_LEVELS):
        owned.append(upward(owned[-1]))
    framed_levels = [framing(owned[k]) for k in range(HALO_LEVELS)]
    coarse_own = owned[HALO_LEVELS]
    channels, coarse_y, coarse_x = coarse_own.shape
    collected = lax.all_gather(coarse_own[None], ("cell", "level"), axis=0, tiled=True)
    coarse_grid = collected.reshape(cell_count, level_count, channels, coarse_y, coarse_x)
    coarse_grid = coarse_grid.transpose(2, 1, 3, 0, 4).reshape(
        channels, level_count * coarse_y, cell_count * coarse_x
    )
    coarse_fields = [coarse_grid]
    top_level = min(cell_count * cells_x, level_count * cells_y).bit_length() - 1
    for k in range(HALO_LEVELS + 1, top_level + 1):
        coarse_fields.append(upward(coarse_fields[-1]))
    local_field = top_far(coarse_fields[-1])
    for index in range(len(coarse_fields) - 2, -1, -1):
        level_field = coarse_fields[index]
        padded = jnp.pad(level_field, ((0, 0), (3, 3), (3, 3)))
        local_field = grouped_far(padded, 3, level_field.shape[1], level_field.shape[2]) + downward(
            local_field
        )
    local_field = lax.dynamic_slice(
        local_field,
        (0, lax.axis_index("level") * coarse_y, lax.axis_index("cell") * coarse_x),
        (channels, coarse_y, coarse_x),
    )
    for k in range(HALO_LEVELS - 1, -1, -1):
        level_field = owned[k]
        local_field = grouped_far(
            framed_levels[k], 3, level_field.shape[1], level_field.shape[2]
        ) + downward(local_field)
    far_real, far_imag = evaluate(local_field, particles[0], particles[1])
    slot_count = framed.shape[1]
    slot_base = lax.axis_index("rep") * half_slots
    target_slots = slot_base + jnp.arange(half_slots, dtype=jnp.int32)
    keep_mask = (target_slots[:, None] != jnp.arange(slot_count, dtype=jnp.int32)[None, :]).astype(
        jnp.float32
    )[:, :, None, None]
    band_rows = 8

    def near_band(row_start):
        target = lax.dynamic_slice_in_dim(particles, row_start, band_rows, 2)
        real_sum = jnp.zeros((half_slots, band_rows, cells_x), jnp.float32)
        imag_sum = jnp.zeros((half_slots, band_rows, cells_x), jnp.float32)
        for step_y in (-1, 0, 1):
            row_band = lax.dynamic_slice_in_dim(framed, row_start + 1 + step_y, band_rows, 2)
            for step_x in (-1, 0, 1):
                source = row_band[:, :, :, 1 + step_x : 1 + step_x + cells_x]
                gap_x = target[0][:, None] - source[0][None] - step_x
                gap_y = target[1][:, None] - source[1][None] - step_y
                weight = source[2][None] / (gap_x * gap_x + gap_y * gap_y + blob_square)
                if step_x == 0 and step_y == 0:
                    weight = weight * keep_mask
                real_sum = real_sum + jnp.sum(weight * gap_x, axis=1)
                imag_sum = imag_sum - jnp.sum(weight * gap_y, axis=1)
        return jnp.stack([real_sum, imag_sum])

    starts = jnp.arange(0, cells_y, band_rows, dtype=jnp.int32)
    bands = lax.map(near_band, starts)
    near = bands.transpose(1, 2, 0, 3, 4).reshape(2, half_slots, cells_y, cells_x)
    real_part = near[0] + far_real
    imag_part = near[1] + far_imag
    return jnp.stack([imag_part, real_part]) / (2.0 * math.pi)


def solution(mesh):
    return jax.shard_map(
        local,
        mesh=mesh,
        in_specs=(
            P(None, "rep", "level", "cell"),
            P("rep", "level", "cell"),
            P(None, "rep", "level", "cell"),
            P("rep", "level", "cell"),
            P("rep", "level", "cell"),
            P("rep", "level", "cell"),
            P("rep", "level", "cell"),
        ),
        out_specs=P(None, "rep", "level", "cell"),
        check_vma=False,
    )
```

profile of v0, /device:TPU:0, one launch (start us, length us, event | category | flops | bytes accessed | tf_op | source)
XLA Modules:
  0.0 1253.7 jit_solution(15650942823292022477)
XLA Ops:
  14.8 16.1 %scatter_custom_fusion.1 = s32[16384]{0:T(1024)} fusion(s32[4096]{0:T(1024)S(1)} %broadcast_select_fusion.1, s32[4096]{0:T(1024)S(1)} %bitcast.975, s32[]{:T(128)} %constant.220.clone.1), kind=kCustom, calls=%fused_computation.410 | custom fusion | bytes 65540
  31.0 8.0 all-to-all-start
  41.9 14.7 %scatter_custom_fusion.2 = f32[3,16384]{0,1:T(8,128)} fusion(s32[4096]{0:T(1024)S(1)} %broadcast_select_fusion, f32[4096,3]{1,0:T(8,128)} %copy.2074, f32[]{:T(128)} %constant.218.clone.1), kind=kCustom, calls=%fused_computation.103 | custom fusion | bytes 197120
  56.5 5.9 copy.2075
  63.4 16.0 %copy.2076 = f32[3,65536]{0,1:T(8,128)} copy(f32[3,65536]{1,0:T(4,128)S(1)} %pad_maximum_fusion.1) | data formatting | bytes 1572864 | tf_op jit(solution)/shard_map/concatenate | solution.py:197
  79.9 7.2 all-to-all-start.1
  87.2 8.6 all-to-all-done.1
  95.8 5.0 copy.2077
  100.8 62.4 %scatter_fusion = f32[3,65536]{0,1:T(8,128)} fusion(f32[3,65536]{0,1:T(8,128)} %copy.2076, s32[16384]{0:T(1024)S(1)} %bitcast.957, f32[16384,3]{1,0:T(8,128)} %copy.2077), kind=kCustom, calls=%fused_computation | custom fusion | bytes 655360 | tf_op jit(solution)/shard_map/scatter | solution.py:198
  163.2 20.2 %copy.2589 = f32[3,16,32,128]{3,2,1,0:T(8,128)} copy(f32[3,16,32,128]{0,3,2,1:T(8,128)} %bitcast.912) | data formatting | bytes 1572864 | tf_op jit(solution)/shard_map/reshape | solution.py:199
  183.5 34.8 %slice_reduce_fusion.1 = (f32[65536]{0:T(1024)}, f32[65536]{0:T(1024)}) fusion(f32[3,65536]{0,1:T(8,128)} %scatter_fusion), kind=kLoop, calls=%fused_computation.102 | loop fusion | bytes 1048576 | tf_op jit(solution)/shard_map/slice | solution.py:236
  248.4 191.3 %all-gather = f32[1280,2,8]{2,1,0:T(2,128)} all-gather(f32[20,2,8]{2,1,0:T(2,128)S(1)} %copy.2384), channel_id=2, replica_groups=mesh['cell'=16,'level'=4,'rep'=2] {'cell','level'}, dimensions={0}, use_global_device_ids=true | all-gather | bytes 83200 | tf_op jit(solution)/shard_map/all_gather | solution.py:210
  613.8 5.2 collective-permute-start
  650.6 5.2 collective-permute-start.14
  670.6 5.1 collective-permute-start.10
  697.1 5.2 collective-permute-start.6
  753.3 5.2 collective-permute-start.2
  1040.1 9.6 concatenate.134
  1049.7 9.6 concatenate.135
  1059.2 9.6 concatenate.136
  1068.8 9.7 concatenate.137
  1078.6 5.7 convolution_bitcast_fusion.7
  1133.0 5.0 pad_maximum_fusion
  1138.0 103.7 %while.16 = (s32[]{:T(128)}, f32[4,2,16,8,128]{4,3,2,1,0:T(8,128)}, s32[4]{0:T(128)}, f32[3,32,34,130]{3,2,1,0:T(8,128)}, f32[3,16,32,128]{3,2,1,0:T(8,128)}, /*...) while((s32[]{:T(128)}, f32[4,2,16,8,128]{4,3,2,1,0:T(8,128)}, ...), condition=%wide.region_25.26_spmd.clone, body=%wide.region_6.25_spmd.clone.sunk | while | flops 58737680 | bytes 14422976 | solution.py:263
  1143.6 7.4 dynamic-slice_bitcast_fusion.31
  1158.2 5.1 fusion.384
  1169.7 7.1 dynamic-slice_bitcast_fusion.31
  1184.0 5.1 fusion.384
  1195.5 7.3 dynamic-slice_bitcast_fusion.31
  1210.0 5.1 fusion.384
  1221.5 7.2 dynamic-slice_bitcast_fusion.31
  1235.8 5.1 fusion.384
  (997 shorter events, 698.2 us)
Async XLA Ops:
  31.0 48.9 %all-to-all-start = ((s32[1,16,1024]{2,0,1:T(1,128)}), s32[1,16,1024]{2,0,1:T(1,128)S(1)}, u32[]{:S(2)}, u32[]{:S(2)}) async-start(s32[1,16,1024]{2,0,1:T(1,128)} %bitcast.8), calls=%async_computation | async-start | bytes 131072 | tf_op jit(solution)/shard_map/all_to_all | solution.py:195
  79.9 15.9 %all-to-all-start.1 = ((f32[3,16,1024]{2,0,1:T(4,128)}), f32[3,16,1024]{2,0,1:T(4,128)S(1)}, u32[]{:S(2)}, u32[]{:S(2)}) async-start(f32[3,16,1024]{2,0,1:T(4,128)} %copy.2075), calls=%async_computation.1 | async-start | bytes 524288 | tf_op jit(solution)/shard_map/all_to_all | solution.py:194
  87.1 131.1 %all-gather.3.cloned.1.call-start = ((), (), s32[]{:S(2)}) async-start(), calls=%async_computation.2 | async-start | bytes 2359296 | tf_op jit(solution)/shard_map/all_gather | solution.py:200
  236.4 396.8 %copy-start.9 = (f32[20,16,64]{2,0,1:T(8,128)}, f32[20,16,64]{2,0,1:T(8,128)S(1)}, u32[]{:S(2)}) copy-start(f32[20,16,64]{2,0,1:T(8,128)S(1)} %fusion.27) | copy-start | bytes 245764
  247.3 195.2 %copy-start.42 = (f32[20,4,16]{0,2,1:T(8,128)}, f32[20,4,16]{0,2,1:T(8,128)S(1)}, u32[]{:S(2)}) copy-start(f32[20,4,16]{0,2,1:T(8,128)S(1)} %fusion.30) | copy-start | bytes 15364
  472.5 37.2 %copy-start.90 = (f32[20,20,1]{1,0,2:T(8,128)S(1)}, f32[20,20,1]{1,0,2:T(8,128)}, u32[]{:S(2)}) copy-start(f32[20,20,1]{1,0,2:T(8,128)} %constant.303) | copy-start | bytes 4804
  472.5 37.4 %copy-start.87 = (f32[20,20,1]{1,0,2:T(8,128)S(1)}, f32[20,20,1]{1,0,2:T(8,128)}, u32[]{:S(2)}) copy-start(f32[20,20,1]{1,0,2:T(8,128)} %constant.310) | copy-start | bytes 4804
  472.5 37.7 %copy-start.86 = (f32[20,20,1]{1,0,2:T(8,128)S(1)}, f32[20,20,1]{1,0,2:T(8,128)}, u32[]{:S(2)}) copy-start(f32[20,20,1]{1,0,2:T(8,128)} %constant.309) | copy-start | bytes 4804
  472.5 38.0 %copy-start.36 = (f32[20,540,1]{1,0,2:T(8,128)S(1)}, f32[20,540,1]{1,0,2:T(8,128)}, u32[]{:S(2)}) copy-start(f32[20,540,1]{1,0,2:T(8,128)} %constant.299) | copy-start | bytes 129604
  473.7 37.4 %copy-start.34 = (f32[20,540,1]{1,0,2:T(8,128)S(1)}, f32[20,540,1]{1,0,2:T(8,128)}, u32[]{:S(2)}) copy-start(f32[20,540,1]{1,0,2:T(8,128)} %constant.300) | copy-start | bytes 129604
  473.7 37.9 %copy-start.32 = (f32[20,540,1]{1,0,2:T(8,128)S(1)}, f32[20,540,1]{1,0,2:T(8,128)}, u32[]{:S(2)}) copy-start(f32[20,540,1]{1,0,2:T(8,128)} %constant.301) | copy-start | bytes 129604
  473.7 38.4 %copy-start.31 = (f32[20,540,1]{1,0,2:T(8,128)S(1)}, f32[20,540,1]{1,0,2:T(8,128)}, u32[]{:S(2)}) copy-start(f32[20,540,1]{1,0,2:T(8,128)} %constant.302) | copy-start | bytes 129604
  582.2 21.8 %collective-permute-start.16 = (f32[20,4,3]{0,2,1:T(4,128)S(1)}, f32[20,4,3]{0,2,1:T(4,128)S(1)}, u32[]{:S(2)}, u32[]{:S(2)}) collective-permute-start(f32[20,4,3]{0,2,1:T(4,128)S(1)} %get-tuple-element.364), channel_id=1, source_target_pairs={{0,8},{8,16},{16,24},{24,32},{32,40},{40,48},{48,56},{56,64},{64,7... | collective-permute-start | bytes 2888 | tf_op jit(solution)/shard_map/ppermute | solution.py:25
  583.5 21.8 %collective-permute-start.17 = (f32[20,4,3]{0,2,1:T(4,128)S(1)}, f32[20,4,3]{0,2,1:T(4,128)S(1)}, u32[]{:S(2)}, u32[]{:S(2)}) collective-permute-start(f32[20,4,3]{0,2,1:T(4,128)S(1)} %get-tuple-element.365), channel_id=1, source_target_pairs={{8,0},{16,8},{24,16},{32,24},{40,32},{48,40},{56,48},{64,56},{72,6... | collective-permute-start | bytes 2888 | tf_op jit(solution)/shard_map/ppermute | solution.py:26
  584.8 27.1 %collective-permute-start.12 = (f32[20,8,3]{2,0,1:T(8,128)S(1)}, f32[20,8,3]{2,0,1:T(8,128)S(1)}, u32[]{:S(2)}, u32[]{:S(2)}) collective-permute-start(f32[20,8,3]{2,0,1:T(8,128)S(1)} %get-tuple-element.360), channel_id=1, source_target_pairs={{0,8},{8,16},{16,24},{24,32},{32,40},{40,48},{48,56},{56,64},{64,7... | collective-permute-start | bytes 5768 | tf_op jit(solution)/shard_map/ppermute | solution.py:25
  589.3 23.8 %collective-permute-start.13 = (f32[20,8,3]{2,0,1:T(8,128)}, f32[20,8,3]{2,0,1:T(8,128)S(1)}, u32[]{:S(2)}, u32[]{:S(2)}) collective-permute-start(f32[20,8,3]{2,0,1:T(8,128)} %get-tuple-element.361), channel_id=1, source_target_pairs={{8,0},{16,8},{24,16},{32,24},{40,32},{48,40},{56,48},{64,56},{72,6... | collective-permute-start | bytes 5768 | tf_op jit(solution)/shard_map/ppermute | solution.py:26
  590.6 39.2 %collective-permute-start.8 = (f32[20,16,3]{2,0,1:T(8,128)}, f32[20,16,3]{2,0,1:T(8,128)S(1)}, u32[]{:S(2)}, u32[]{:S(2)}) collective-permute-start(f32[20,16,3]{2,0,1:T(8,128)} %get-tuple-element.356), channel_id=1, source_target_pairs={{0,8},{8,16},{16,24},{24,32},{32,40},{40,48},{48,56},{56,64},{64,7... | collective-permute-start | bytes 11528 | tf_op jit(solution)/shard_map/ppermute | solution.py:25
  603.9 27.8 %collective-permute-start.9 = (f32[20,16,3]{2,0,1:T(8,128)}, f32[20,16,3]{2,0,1:T(8,128)}, u32[]{:S(2)}, u32[]{:S(2)}) collective-permute-start(f32[20,16,3]{2,0,1:T(8,128)} %get-tuple-element.357), channel_id=1, source_target_pairs={{8,0},{16,8},{24,16},{32,24},{40,32},{48,40},{56,48},{64,56},{72,6... | collective-permute-start | bytes 11528 | tf_op jit(solution)/shard_map/ppermute | solution.py:26
  605.3 63.4 %collective-permute-start.4 = (f32[20,32,3]{2,1,0:T(8,128)}, f32[20,32,3]{2,1,0:T(8,128)S(1)}, u32[]{:S(2)}, u32[]{:S(2)}) collective-permute-start(f32[20,32,3]{2,1,0:T(8,128)} %get-tuple-element.352), channel_id=1, source_target_pairs={{0,8},{8,16},{16,24},{24,32},{32,40},{40,48},{48,56},{56,64},{64,7... | collective-permute-start | bytes 23048 | tf_op jit(solution)/shard_map/ppermute | solution.py:25
  611.9 58.0 %collective-permute-start.5 = (f32[20,32,3]{2,1,0:T(8,128)}, f32[20,32,3]{2,1,0:T(8,128)S(1)}, u32[]{:S(2)}, u32[]{:S(2)}) collective-permute-start(f32[20,32,3]{2,1,0:T(8,128)} %get-tuple-element.353), channel_id=1, source_target_pairs={{8,0},{16,8},{24,16},{32,24},{40,32},{48,40},{56,48},{64,56},{72,6... | collective-permute-start | bytes 23048 | tf_op jit(solution)/shard_map/ppermute | solution.py:26
  613.8 131.5 %collective-permute-start = (f32[3,32,32,1]{2,1,3,0:T(8,128)}, f32[3,32,32,1]{2,1,3,0:T(8,128)}, u32[]{:S(2)}, u32[]{:S(2)}) collective-permute-start(f32[3,32,32,1]{2,1,3,0:T(8,128)} %copy.2079), channel_id=1, source_target_pairs={{0,8},{8,16},{16,24},{24,32},{32,40},{40,48},{48,56},{56,64},{64,7... | collective-permute-start | bytes 36872 | tf_op jit(solution)/shard_map/ppermute | solution.py:25
  629.8 19.5 %collective-permute-start.18 = (f32[20,3,22]{0,2,1:T(8,128)}, f32[20,3,22]{0,2,1:T(8,128)}, u32[]{:S(2)}, u32[]{:S(2)}) collective-permute-start(f32[20,3,22]{0,2,1:T(8,128)} %get-tuple-element.362), channel_id=1, source_target_pairs={{0,2},{2,4},{4,6},{1,3},{3,5},{5,7},{8,10},{10,12},{12,14},{9,11},... | collective-permute-start | bytes 15848 | tf_op jit(solution)/shard_map/ppermute | solution.py:25
  631.7 18.9 %collective-permute-start.19 = (f32[20,3,22]{0,2,1:T(8,128)}, f32[20,3,22]{0,2,1:T(8,128)}, u32[]{:S(2)}, u32[]{:S(2)}) collective-permute-start(f32[20,3,22]{0,2,1:T(8,128)} %get-tuple-element.363), channel_id=1, source_target_pairs={{2,0},{4,2},{6,4},{3,1},{5,3},{7,5},{10,8},{12,10},{14,12},{11,9},... | collective-permute-start | bytes 15848 | tf_op jit(solution)/shard_map/ppermute | solution.py:26
  649.3 98.9 %collective-permute-start.1 = (f32[3,32,32,1]{2,1,3,0:T(8,128)}, f32[3,32,32,1]{2,1,3,0:T(8,128)}, u32[]{:S(2)}, u32[]{:S(2)}) collective-permute-start(f32[3,32,32,1]{2,1,3,0:T(8,128)} %copy.2080), channel_id=1, source_target_pairs={{8,0},{16,8},{24,16},{32,24},{40,32},{48,40},{56,48},{64,56},{72,6... | collective-permute-start | bytes 36872 | tf_op jit(solution)/shard_map/ppermute | solution.py:26
  650.6 45.2 %collective-permute-start.14 = (f32[20,3,38]{2,0,1:T(8,128)}, f32[20,3,38]{2,0,1:T(8,128)}, u32[]{:S(2)}, u32[]{:S(2)}) collective-permute-start(f32[20,3,38]{2,0,1:T(8,128)} %get-tuple-element.358), channel_id=1, source_target_pairs={{0,2},{2,4},{4,6},{1,3},{3,5},{5,7},{8,10},{10,12},{12,14},{9,11},... | collective-permute-start | bytes 27368 | tf_op jit(solution)/shard_map/ppermute | solution.py:25
  668.6 28.5 %collective-permute-start.15 = (f32[20,3,38]{2,0,1:T(8,128)}, f32[20,3,38]{2,0,1:T(8,128)S(1)}, u32[]{:S(2)}, u32[]{:S(2)}) collective-permute-start(f32[20,3,38]{2,0,1:T(8,128)} %get-tuple-element.359), channel_id=1, source_target_pairs={{2,0},{4,2},{6,4},{3,1},{5,3},{7,5},{10,8},{12,10},{14,12},{11,9},... | collective-permute-start | bytes 27368 | tf_op jit(solution)/shard_map/ppermute | solution.py:26
  670.6 88.5 %collective-permute-start.10 = (f32[20,3,70]{2,0,1:T(8,128)}, f32[20,3,70]{2,0,1:T(8,128)}, u32[]{:S(2)}, u32[]{:S(2)}) collective-permute-start(f32[20,3,70]{2,0,1:T(8,128)} %get-tuple-element.354), channel_id=1, source_target_pairs={{0,2},{2,4},{4,6},{1,3},{3,5},{5,7},{8,10},{10,12},{12,14},{9,11},... | collective-permute-start | bytes 50408 | tf_op jit(solution)/shard_map/ppermute | solution.py:25
  695.8 64.6 %collective-permute-start.11 = (f32[20,3,70]{2,0,1:T(8,128)}, f32[20,3,70]{2,0,1:T(8,128)}, u32[]{:S(2)}, u32[]{:S(2)}) collective-permute-start(f32[20,3,70]{2,0,1:T(8,128)} %get-tuple-element.355), channel_id=1, source_target_pairs={{2,0},{4,2},{6,4},{3,1},{5,3},{7,5},{10,8},{12,10},{14,12},{11,9},... | collective-permute-start | bytes 50408 | tf_op jit(solution)/shard_map/ppermute | solution.py:26
  697.1 201.4 %collective-permute-start.6 = (f32[20,3,134]{2,1,0:T(4,128)}, f32[20,3,134]{2,1,0:T(4,128)}, u32[]{:S(2)}, u32[]{:S(2)}) collective-permute-start(f32[20,3,134]{2,1,0:T(4,128)} %get-tuple-element.348), channel_id=1, source_target_pairs={{0,2},{2,4},{4,6},{1,3},{3,5},{5,7},{8,10},{10,12},{12,14},{9,11},... | collective-permute-start | bytes 96488 | tf_op jit(solution)/shard_map/ppermute | solution.py:25
  745.3 153.2 %collective-permute-start.7 = (f32[20,3,134]{2,1,0:T(4,128)}, f32[20,3,134]{2,1,0:T(4,128)}, u32[]{:S(2)}, u32[]{:S(2)}) collective-permute-start(f32[20,3,134]{2,1,0:T(4,128)} %get-tuple-element.349), channel_id=1, source_target_pairs={{2,0},{4,2},{6,4},{3,1},{5,3},{7,5},{10,8},{12,10},{14,12},{11,9},... | collective-permute-start | bytes 96488 | tf_op jit(solution)/shard_map/ppermute | solution.py:26
  753.3 377.6 %collective-permute-start.2 = (f32[3,32,1,130]{3,1,2,0:T(8,128)}, f32[3,32,1,130]{3,1,2,0:T(8,128)}, u32[]{:S(2)}, u32[]{:S(2)}) collective-permute-start(f32[3,32,1,130]{3,1,2,0:T(8,128)} %copy.2083), channel_id=1, source_target_pairs={{0,2},{2,4},{4,6},{1,3},{3,5},{5,7},{8,10},{10,12},{12,14},{9,11},... | collective-permute-start | bytes 149768 | tf_op jit(solution)/shard_map/ppermute | solution.py:25
  759.1 372.8 %collective-permute-start.3 = (f32[3,32,1,130]{3,1,2,0:T(8,128)}, f32[3,32,1,130]{3,1,2,0:T(8,128)}, u32[]{:S(2)}, u32[]{:S(2)}) collective-permute-start(f32[3,32,1,130]{3,1,2,0:T(8,128)} %copy.2084), channel_id=1, source_target_pairs={{2,0},{4,2},{6,4},{3,1},{5,3},{7,5},{10,8},{12,10},{14,12},{11,9},... | collective-permute-start | bytes 149768 | tf_op jit(solution)/shard_map/ppermute | solution.py:26
  (125 other events, 1228.2 us)
Sparse Core Ops, SparseCore 0:
  183.6 10.0 all-gather.2
where the time goes:
time: 1270 us; the launch traced here: 1250 us
  local copies, waits for them, and re-layouts  763 us (60%)
  blocking collectives  191 us (15%)
  matrix products  96.1 us (8%)
  other arithmetic  82.5 us (6%)
  starting transfers between devices  71 us (6%)
  loops' own time  23 us (2%)
  between operations  17.8 us (1%)
    slice x305, local copies, waits for them, and re-layouts, grouped_far(): padded[:, first_y:first_y + cells_y:2, first_x:first_x + cells_x:2]  335 us
    all_gather x1, blocking collectives, local(): lax.all_gather(coarse_own[None], ('cell', 'level'), axis=0, tiled=True)  191 us
    dot_general x96, matrix products, apply_matrix(): jnp.einsum('ij,jyx->iyx', jnp.asarray(matrix, dtype=jnp.float32), level_f...  89.4 us
    unnamed x315, local copies, waits for them, and re-layouts  80.3 us
    concatenate x28, local copies, waits for them, and re-layouts, grouped_far(): jnp.concatenate(pieces, axis=0)  77.2 us
    scatter x1, local copies, waits for them, and re-layouts, local(): resident.at[:, arrived_at.reshape(-1)]  62.4 us
    ppermute x10, starting transfers between devices, with_halo(): before = lax.ppermute(last, axis, up)  42.7 us
    reduce_sum x8, other arithmetic, near_band(): real_sum = real_sum + jnp.sum(weight * gap_x, axis=1)  36.7 us
  transfers between devices with their start and end apart: 23, of which 1 were waited for; matrix products, arithmetic and copies ran while one was open for 45% of the time, Pallas kernels for 0%

commit v1 on v0

v1 whole, which is shorter than its diff:
```python
import functools
import math

import jax
import jax.numpy as jnp
import numpy as np
from jax import lax
from jax.experimental import pallas as pl
from jax.experimental.pallas import tpu as pltpu
from jax.sharding import PartitionSpec as P

ORDER = 10
CHAN = 2 * ORDER
FAMILY = 4 * CHAN
CAP = 1024
BLOB = 0.09
LANES = 128
HEIGHTS = (16, 8, 4, 2, 1)
WIDTHS = (64, 32, 16, 8, 4)
OFFSETS = (0, 16, 24, 28, 30)
ROWS = 31
PACKS = (None, 0, 34, 52, 62)
VMEM = 56 * 2**20

f32 = jnp.float32
bf16 = jnp.bfloat16
precise = lax.Precision.HIGHEST


def real_form(matrix):
    top_rows = np.concatenate([matrix.real, -matrix.imag], axis=1)
    low_rows = np.concatenate([matrix.imag, matrix.real], axis=1)
    return np.concatenate([top_rows, low_rows], axis=0)


def child_offset(parity_x, parity_y):
    return complex((parity_x - 0.5) / 2.0, (parity_y - 0.5) / 2.0)


def upward_table(parity_x, parity_y):
    offset = child_offset(parity_x, parity_y)
    matrix = np.zeros((ORDER, ORDER), complex)
    for k in range(ORDER):
        for m in range(k + 1):
            matrix[k, m] = math.comb(k, m) * 0.5**m * offset ** (k - m)
    return real_form(matrix)


def downward_table(parity_x, parity_y):
    offset = child_offset(parity_x, parity_y)
    matrix = np.zeros((ORDER, ORDER), complex)
    for m in range(ORDER):
        for l in range(m, ORDER):
            matrix[m, l] = 0.5 ** (m + 1) * math.comb(l, m) * offset ** (l - m)
    return real_form(matrix)


def far_table(step_x, step_y):
    distance = complex(step_x, step_y)
    matrix = np.zeros((ORDER, ORDER), complex)
    for l in range(ORDER):
        for k in range(ORDER):
            matrix[l, k] = (-1) ** (k + 1) * math.comb(k + l, l) * distance ** (-(k + l + 1))
    return real_form(matrix)


def family(parity_x, parity_y):
    first = (2 * parity_x + parity_y) * CHAN
    return slice(first, first + CHAN)


def upward_family():
    table = np.zeros((CHAN, FAMILY))
    for b in (0, 1):
        for a in (0, 1):
            table[:, family(b, a)] = upward_table(b, a)
    return table


def downward_family():
    table = np.zeros((FAMILY, CHAN))
    for b in (0, 1):
        for a in (0, 1):
            table[family(b, a), :] = downward_table(b, a)
    return table


def far_family():
    table = np.zeros((3, FAMILY, 3, FAMILY))
    for dx in (-1, 0, 1):
        for dy in (-1, 0, 1):
            for bt in (0, 1):
                for at in (0, 1):
                    for bs in (0, 1):
                        for as_ in (0, 1):
                            step_x = 2 * dx + bs - bt
                            step_y = 2 * dy + as_ - at
                            if max(abs(step_x), abs(step_y)) >= 2:
                                table[dx + 1, family(bt, at), dy + 1, family(bs, as_)] = far_table(
                                    step_x, step_y
                                )
    return table.reshape(3 * FAMILY, 3 * FAMILY)


def coarse_tables():
    far5 = {}
    to_top = np.zeros((4, LANES, LANES))
    near5 = np.zeros((4, 12, LANES, LANES))
    from_top = np.zeros((4, LANES, LANES))
    lane = lambda column: np.arange(CHAN) * 4 + column
    for row in range(4):
        for column in range(4):
            lift = upward_table(column // 2, row // 2) @ upward_table(column % 2, row % 2)
            to_top[row][np.ix_(lane(column), np.arange(CHAN))] = lift.T
            drop = downward_table(column % 2, row % 2) @ downward_table(column // 2, row // 2)
            from_top[row][np.ix_(np.arange(CHAN), lane(column))] = drop.T
    for row in range(4):
        for column in range(4):
            down = downward_table(column % 2, row % 2)
            x = 4 + column
            for step in range(3):
                for other_row in range(4):
                    for other in range(4):
                        u = 4 * step + other
                        total = np.zeros((CHAN, CHAN))
                        if abs(u // 2 - x // 2) <= 1:
                            if max(abs(u - x), abs(other_row - row)) >= 2:
                                total += far_table(u - x, other_row - row)
                        if abs(u // 2 - x // 2) >= 2:
                            key = (u // 2 - x // 2, other_row // 2 - row // 2)
                            if key not in far5:
                                far5[key] = far_table(*key)
                            total += down @ far5[key] @ upward_table(other % 2, other_row % 2)
                        near5[row, step * 4 + other_row][np.ix_(lane(other), lane(column))] += total.T
    top = np.zeros((LANES, 32 * 32))
    for step in range(-15, 16):
        if abs(step) >= 2:
            top[:CHAN, (step + 15) * 32 : (step + 15) * 32 + CHAN] = far_table(step, 0).T
    return to_top, near5, from_top, top


def halves_np(table):
    high = np.asarray(table, np.float32).astype(jnp.bfloat16)
    low = (np.asarray(table, np.float32) - high.astype(np.float32)).astype(jnp.bfloat16)
    return high, low


def split_lanes():
    table = np.zeros((LANES, LANES), np.float32)
    x = np.arange(LANES)
    table[x, 64 * (x % 2) + x // 2] = 1.0
    return np.concatenate([table, table], axis=0).astype(jnp.bfloat16)


def join_lanes():
    table = np.zeros((2, LANES, LANES), np.float32)
    x = np.arange(64)
    table[0, x, 2 * x] = 1.0
    table[1, x, 2 * x + 1] = 1.0
    table = table.reshape(2 * LANES, LANES)
    return np.concatenate([table, table], axis=0).astype(jnp.bfloat16)


def quarter_lanes():
    k = np.arange(LANES)
    return (k[:, None] % 4 == k[None, :]).astype(np.float32)


def halves(value):
    high = value.astype(bf16)
    return high, (value - high.astype(f32)).astype(bf16)


def dot(left, right):
    return jnp.dot(left, right, preferred_element_type=f32)


def lane_index(rows):
    return lax.broadcasted_iota(jnp.int32, (rows, LANES), 1)


def whole(shape):
    return pl.BlockSpec(shape, lambda *_: (0,) * len(shape))


def upward_kernel(
    own, other, split_ref, lift_ref, spread_ref, cells, packed, coarse, mom, raw
):
    for tile in range(4):
        rows = pl.ds(8 * tile, 8)

        def add_slot(j, sums):
            for ref in (own, other):
                x, y, re = ref[0, j, rows, :], ref[1, j, rows, :], ref[2, j, rows, :]
                real, imag = list(sums[:ORDER]), list(sums[ORDER:])
                real[0] = real[0] + re
                im = re * y
                re = re * x
                real[1] = real[1] + re
                imag[1] = imag[1] + im
                for k in range(2, ORDER):
                    re, im = re * x - im * y, re * y + im * x
                    real[k] = real[k] + re
                    imag[k] = imag[k] + im
                sums = tuple(real + imag)
            return sums

        sums = lax.fori_loop(
            0, 16, add_slot, tuple(jnp.zeros((8, LANES), f32) for _ in range(CHAN)), unroll=2
        )
        for c in range(CHAN):
            mom[pl.ds(8 * tile * CHAN + c, 8, stride=CHAN), :] = sums[c]

    lane40 = lane_index(40)
    lane80 = lane_index(FAMILY)
    first = jnp.zeros((FAMILY, LANES), f32)
    last = jnp.zeros((FAMILY, LANES), f32)
    for k, height in enumerate(HEIGHTS):
        source = mom[...] if k == 0 else raw[pl.ds(0, 40 * height), :]
        spread = dot(jnp.concatenate(halves(source), axis=1), split_ref[...])
        parents = []
        for row in range(height):
            block = spread[40 * row : 40 * row + 40]
            even = jnp.where(lane40 < 64, block, 0.0)
            odd = jnp.where(lane40 < 64, pltpu.roll(block, 64, 1), 0.0)
            parent = jnp.concatenate([even, odd], axis=0)
            index = OFFSETS[k] + row
            cells[pl.ds(FAMILY * index, FAMILY), :] = parent
            first = jnp.where(lane80 == index, pltpu.roll(parent, index, 1), first)
            last = jnp.where(
                lane80 == index, pltpu.roll(parent, (index - WIDTHS[k] + 1) % LANES, 1), last
            )
            parents.append(parent)
        high, low = halves(jnp.concatenate(parents, axis=1))
        lifted = dot(lift_ref[...], jnp.concatenate([high, low, high], axis=0))
        for row in range(height):
            raw[pl.ds(CHAN * row, CHAN), :] = lifted[:CHAN, LANES * row : LANES * (row + 1)]
    packed[0, pl.ds(32, FAMILY), :] = first
    packed[1, pl.ds(32, FAMILY), :] = last

    four = jnp.dot(raw[pl.ds(0, 24), :], spread_ref[...], precision=precise)
    row24 = lax.broadcasted_iota(jnp.int32, (24, LANES), 0)
    line = jnp.sum(jnp.where((lane_index(24) // 4 == row24) & (row24 < CHAN), four, 0.0), axis=0, keepdims=True)
    coarse[...] = jnp.broadcast_to(line, coarse.shape)

    lane32 = lane_index(32)

    def edge(j, sides):
        left, right = sides
        for half, ref in enumerate((own, other)):
            for comp in range(3):
                m = comp * 32 + half * 16 + j
                value = ref[comp, j]
                left = jnp.where(lane32 == m, pltpu.roll(value, m, 1), left)
                right = jnp.where(lane32 == m, pltpu.roll(value, m + 1, 1), right)
        return left, right

    zero = jnp.zeros((32, LANES), f32)
    left, right = lax.fori_loop(0, 16, edge, (zero, zero))
    packed[0, pl.ds(0, 32), :] = left
    packed[1, pl.ds(0, 32), :] = right


def ring_columns(parent, k, index, from_left, from_right, lane):
    width = WIDTHS[k]
    parent = jnp.where(lane == LANES - 1, pltpu.roll(from_left, (LANES - 1 - index) % LANES, 1), parent)
    return jnp.where(lane == width, pltpu.roll(from_right, (width - index) % LANES, 1), parent)


def rows_kernel(own, other, cells, from_left, from_right, out):
    lane80 = lane_index(FAMILY)
    left, right = from_left[pl.ds(32, FAMILY), :], from_right[pl.ds(32, FAMILY), :]
    for side in (0, 1):
        row = 31 * side
        for comp in range(3):
            for half, ref in enumerate((own, other)):
                for j in range(16):
                    out[side, pl.ds(comp * 32 + half * 16 + j, 1), :] = ref[comp, j, pl.ds(row, 1), :]
        out[side, pl.ds(96, 1), :] = from_left[pl.ds(row, 1), :]
        out[side, pl.ds(97, 1), :] = from_right[pl.ds(row, 1), :]
        out[side, pl.ds(98, 6), :] = jnp.zeros((6, LANES), f32)
        packed = jnp.zeros((FAMILY, LANES), f32)
        for k, height in enumerate(HEIGHTS):
            index = OFFSETS[k] + (height - 1) * side
            parent = cells[pl.ds(FAMILY * index, FAMILY), :]
            parent = ring_columns(parent, k, index, left, right, lane80)
            if k == 0:
                out[side, pl.ds(104, FAMILY), :] = parent
            else:
                moved = pltpu.roll(parent, PACKS[k] + 1, 1)
                inside = (lane80 >= PACKS[k]) & (lane80 < PACKS[k] + WIDTHS[k] + 2)
                packed = jnp.where(inside, moved, packed)
        out[side, pl.ds(104 + FAMILY, FAMILY), :] = packed


GROUP = 8


def near_kernel(own, other, from_left, from_right, above, below, out, src):
    lane32 = lane_index(32)
    lane1 = lane_index(1)

    for comp in range(3):
        for half, ref in enumerate((own, other)):

            def frame(j, _, comp=comp, half=half, ref=ref):
                m = comp * 32 + half * 16 + j
                back = (LANES - m) % LANES if isinstance(m, int) else LANES - m
                value = ref[comp, j]
                rows = (value, above[pl.ds(m, 1), :], below[pl.ds(m, 1), :])
                lefts = (from_left[pl.ds(0, 32), :], above[pl.ds(96, 1), :], below[pl.ds(96, 1), :])
                rights = (from_right[pl.ds(0, 32), :], above[pl.ds(97, 1), :], below[pl.ds(97, 1), :])
                for part in range(3):
                    place = (pl.ds(8, 32), pl.ds(7, 1), pl.ds(40, 1))[part]
                    lane = lane32 if part == 0 else lane1
                    middle = rows[part]
                    before = jnp.where(
                        lane == 0, pltpu.roll(lefts[part], back, 1), pltpu.roll(middle, 1, 1)
                    )
                    after = jnp.where(
                        lane == LANES - 1,
                        pltpu.roll(rights[part], LANES - 1 - m, 1),
                        pltpu.roll(middle, LANES - 1, 1),
                    )
                    if comp == 0:
                        before = before - 1.0
                        after = after + 1.0
                    src[0, m, place, :] = before
                    src[1, m, place, :] = middle
                    src[2, m, place, :] = after
                return 0

            lax.fori_loop(0, 16, frame, 0)

    for tile in range(4):
        for group in range(16 // GROUP):
            tx = [own[0, group * GROUP + i, pl.ds(8 * tile, 8), :] for i in range(GROUP)]
            ty0 = [own[1, group * GROUP + i, pl.ds(8 * tile, 8), :] for i in range(GROUP)]
            acc = tuple(jnp.zeros((8, LANES), f32) for _ in range(2 * GROUP))
            for dy in (-1, 0, 1):
                ty = [value - float(dy) for value in ty0] if dy else ty0
                rows = pl.ds(8 + 8 * tile + dy, 8)
                for dx in range(3):

                    def pairs(j, acc, dx=dx, rows=rows, ty=ty, tx=tx):
                        acc = list(acc)
                        sx, sy, q = src[dx, j, rows, :], src[dx, 32 + j, rows, :], src[dx, 64 + j, rows, :]
                        for i in range(GROUP):
                            gap_x = tx[i] - sx
                            gap_y = ty[i] - sy
                            weight = q * (1.0 / (gap_x * gap_x + (gap_y * gap_y + BLOB)))
                            acc[i] = acc[i] + weight * gap_x
                            acc[GROUP + i] = acc[GROUP + i] + weight * gap_y
                        return tuple(acc)

                    acc = lax.fori_loop(0, 32, pairs, acc, unroll=4)
            for i in range(GROUP):
                out[0, group * GROUP + i, pl.ds(8 * tile, 8), :] = acc[i]
                out[1, group * GROUP + i, pl.ds(8 * tile, 8), :] = acc[GROUP + i]


def far_kernel(
    place, own, near, cells, from_left, from_right, above, below, gathered,
    far_ref, drop_ref, join_ref, spread_ref, to_top, near5, from_top, top_ref,
    out, high, low, fars, paired, joined_ref, loc,
):
    cell = place[0]
    level = place[1]
    tops = jnp.zeros((16, LANES), f32)
    for row in range(4):
        tops = tops + jnp.dot(gathered[pl.ds(row, 16, stride=4), :], to_top[row], precision=precise)
    spread = jnp.dot(tops, top_ref[...], precision=precise)
    source = lax.broadcasted_iota(jnp.int32, (16, 1024), 0)
    step = lax.broadcasted_iota(jnp.int32, (16, 1024), 1) // 32
    line = jnp.sum(jnp.where(step == source - cell + 15, spread, 0.0), axis=0, keepdims=True)
    total = line[:, :LANES]
    for block in range(1, 8):
        total = total + line[:, LANES * block : LANES * (block + 1)]
    total = jnp.broadcast_to(total, (8, LANES))
    total = total + pltpu.roll(total, 64, 1)
    total = total + pltpu.roll(total, 32, 1)
    total = jnp.where(lane_index(8) < CHAN, total, 0.0)
    five = jnp.dot(total, from_top[0], precision=precise)
    for step in range(3):
        there = cell + step - 1
        valid = jnp.where((there >= 0) & (there < 16), 1.0, 0.0)
        there = jnp.clip(there, 0, 15)
        for row in range(4):
            value = jnp.broadcast_to(gathered[pl.ds(there * 4 + row, 1), :], (8, LANES)) * valid
            five = five + jnp.dot(value, near5[0, step * 4 + row], precision=precise)
    five = jnp.broadcast_to(five[0:1], (32, LANES))
    row32 = lax.broadcasted_iota(jnp.int32, (32, LANES), 0)
    five = jnp.where((lane_index(32) // 4 == row32) & (row32 < CHAN), five, 0.0)
    loc[...] = jnp.zeros(loc.shape, f32)
    loc[pl.ds(0, 32), pl.ds(0, LANES)] = jnp.dot(five, spread_ref[...], precision=precise)

    lane80 = lane_index(FAMILY)
    left, right = from_left[pl.ds(32, FAMILY), :], from_right[pl.ds(32, FAMILY), :]
    start = 0
    starts = []
    for k, height in enumerate(HEIGHTS):
        starts.append(start)
        for row in range(-1, height + 1):
            if row in (-1, height):
                ref = above if row == -1 else below
                if k == 0:
                    parent = ref[pl.ds(104, FAMILY), :]
                else:
                    packed = ref[pl.ds(104 + FAMILY, FAMILY), :]
                    parent = pltpu.roll(packed, LANES - PACKS[k] - 1, 1)
                    parent = jnp.where((lane80 <= WIDTHS[k]) | (lane80 == LANES - 1), parent, 0.0)
            else:
                index = OFFSETS[k] + row
                parent = cells[pl.ds(FAMILY * index, FAMILY), :]
                parent = ring_columns(parent, k, index, left, right, lane80)
            part_high, part_low = halves(parent)
            high[pl.ds(FAMILY * start, FAMILY), :] = part_high
            low[pl.ds(FAMILY * start, FAMILY), :] = part_low
            start += 1

    def far_rows(k, rows):
        both = []
        for ref in (high, low):
            both.append(
                jnp.concatenate(
                    [ref[pl.ds(FAMILY * (starts[k] + row), 3 * FAMILY), :] for row in rows], axis=1
                )
            )
        size = 3 * FAMILY
        product = dot(far_ref[...], both[0])
        product = product[:size] + product[size:] + dot(far_ref[pl.ds(0, size), :], both[1])
        for place_, row in enumerate(rows):
            part = product[:, LANES * place_ : LANES * (place_ + 1)]
            fars[pl.ds(FAMILY * (OFFSETS[k] + row), FAMILY), :] = (
                part[FAMILY : 2 * FAMILY]
                + pltpu.roll(part[:FAMILY], 1, 1)
                + pltpu.roll(part[2 * FAMILY :], LANES - 1, 1)
            )

    for k, height in enumerate(HEIGHTS):
        for row in range(0, height, 2):
            far_rows(k, (row, row + 1) if height > 1 else (row,))

    for k in range(4, -1, -1):
        height = HEIGHTS[k]
        part_high, part_low = halves(loc[:, pl.ds(0, LANES * height)])
        dropped = dot(drop_ref[...], jnp.concatenate([part_high, part_low, part_high], axis=0))
        for row in range(height):
            here = dropped[:, LANES * row : LANES * (row + 1)] + fars[pl.ds(FAMILY * (OFFSETS[k] + row), FAMILY), :]
            paired[pl.ds(40 * row, 40), :] = jnp.concatenate([here[:40], here[40:]], axis=1)
        part_high, part_low = halves(paired[pl.ds(0, 40 * height), :])
        joined = dot(jnp.concatenate([part_high, part_low], axis=1), join_ref[...])
        joined_ref[pl.ds(0, 40 * height), :] = joined
        if k > 0:
            for row in range(2 * height):
                loc[pl.ds(0, CHAN), pl.ds(LANES * row, LANES)] = joined_ref[pl.ds(CHAN * row, CHAN), :]

    scale = 1.0 / (2.0 * math.pi)
    for tile in range(4):
        rows = pl.ds(8 * tile, 8)
        terms = [joined_ref[pl.ds(8 * tile * CHAN + c, 8, stride=CHAN), :] for c in range(CHAN)]

        def value(j, _, terms=terms, rows=rows):
            x, y = own[0, j, rows, :], own[1, j, rows, :]
            re, im = terms[ORDER - 1], terms[CHAN - 1]
            for l in range(ORDER - 2, -1, -1):
                re, im = re * x - im * y + terms[l], re * y + im * x + terms[ORDER + l]
            out[0, j, rows, :] = (im - near[1, j, rows, :]) * scale
            out[1, j, rows, :] = (re + near[0, j, rows, :]) * scale
            return 0

        lax.fori_loop(0, 16, value, 0, unroll=2)


def params():
    return pltpu.CompilerParams(vmem_limit_bytes=VMEM)


def shape(*sizes):
    return jax.ShapeDtypeStruct(sizes, f32)


def neighbours(value, axis, step):
    size = lax.axis_size(axis)
    return lax.ppermute(value, axis, [(i, i + step) for i in range(size) if 0 <= i + step < size])


def fields(own):
    other = lax.ppermute(own, "rep", [(0, 1), (1, 0)])
    lift_high, lift_low = halves_np(upward_family())
    lift = np.zeros((32, 3 * FAMILY), jnp.bfloat16)
    lift[:CHAN] = np.concatenate([lift_high, lift_high, lift_low], axis=1)
    cells, packed, coarse = pl.pallas_call(
        upward_kernel,
        out_shape=(shape(ROWS * FAMILY, LANES), shape(2, 32 + FAMILY, LANES), shape(64, LANES)),
        scratch_shapes=[pltpu.VMEM((640, LANES), f32), pltpu.VMEM((320, LANES), f32)],
        compiler_params=params(),
        name="upward",
    )(own, other, jnp.asarray(split_lanes()), jnp.asarray(lift), jnp.asarray(quarter_lanes().T.copy()))
    from_left = neighbours(packed[1], "cell", 1)
    from_right = neighbours(packed[0], "cell", -1)
    gathered = lax.all_to_all(coarse, ("cell", "level"), 0, 0, tiled=True)
    rows = pl.pallas_call(
        rows_kernel,
        out_shape=shape(2, 104 + 2 * FAMILY, LANES),
        compiler_params=params(),
        name="rows",
    )(own, other, cells, from_left, from_right)
    above = neighbours(rows[1], "level", 1)
    below = neighbours(rows[0], "level", -1)
    near = pl.pallas_call(
        near_kernel,
        out_shape=shape(2, 16, 32, LANES),
        scratch_shapes=[pltpu.VMEM((3, 96, 48, LANES), f32)],
        compiler_params=params(),
        name="near",
    )(own, other, from_left, from_right, above, below)
    far_high, far_low = halves_np(far_family())
    drop_table = np.zeros((FAMILY, 32))
    drop_table[:, :CHAN] = downward_family()
    drop_high, drop_low = halves_np(drop_table)
    to_top, near5, from_top, top = coarse_tables()
    tables = [
        np.concatenate([far_high, far_low], axis=0),
        np.concatenate([drop_high, drop_high, drop_low], axis=1),
        join_lanes(),
        quarter_lanes(),
        to_top.astype(np.float32),
        near5.astype(np.float32),
        from_top.astype(np.float32),
        top.astype(np.float32),
    ]
    operands = [own, near, cells, from_left, from_right, above, below, gathered] + [
        jnp.asarray(table) for table in tables
    ]
    specs = [whole(value.shape) for value in operands]
    specs[13] = pl.BlockSpec((1, 12, LANES, LANES), lambda i, place: (place[1], 0, 0, 0))
    specs[14] = pl.BlockSpec((1, LANES, LANES), lambda i, place: (place[1], 0, 0))
    place = jnp.stack([lax.axis_index("cell"), lax.axis_index("level")]).astype(jnp.int32)
    return pl.pallas_call(
        far_kernel,
        grid_spec=pltpu.PrefetchScalarGridSpec(
            num_scalar_prefetch=1,
            grid=(1,),
            in_specs=specs,
            out_specs=whole((2, 16, 32, LANES)),
            scratch_shapes=[
                pltpu.VMEM((41 * FAMILY, LANES), bf16),
                pltpu.VMEM((41 * FAMILY, LANES), bf16),
                pltpu.VMEM((ROWS * FAMILY, LANES), f32),
                pltpu.VMEM((640, 2 * LANES), f32),
                pltpu.VMEM((640, LANES), f32),
                pltpu.VMEM((32, 16 * LANES), f32),
            ],
        ),
        out_shape=shape(2, 16, 32, LANES),
        compiler_params=params(),
        name="far",
    )(place, *operands)


def local(
    resident_pos, resident_strength, mover_pos, mover_strength, mover_owner, mover_leaf, mover_slot
):
    cell_count = lax.axis_size("cell")
    half_slots, cells_y, cells_x = resident_strength.shape
    leaves = cells_y * cells_x
    owner_cell = mover_owner.reshape(-1)
    address = mover_slot.reshape(-1) * leaves + mover_leaf.reshape(-1)
    peer_ids = jnp.arange(cell_count, dtype=jnp.int32)
    onehot = (owner_cell[:, None] == peer_ids[None, :]).astype(jnp.int32)
    rank_in_owner = jnp.sum(jnp.cumsum(onehot, axis=0) * onehot, axis=1) - 1
    values = jnp.concatenate([mover_pos.reshape(2, -1), mover_strength.reshape(1, -1)])
    outgoing = (
        jnp.zeros((3, cell_count, CAP), jnp.float32).at[:, owner_cell, rank_in_owner].set(values)
    )
    addresses = (
        jnp.full((1, cell_count, CAP), half_slots * leaves, jnp.int32)
        .at[0, owner_cell, rank_in_owner]
        .set(address)
    )
    arrived, arrived_at = (
        lax.all_to_all(outgoing, "cell", split_axis=1, concat_axis=1, tiled=True),
        lax.all_to_all(addresses, "cell", split_axis=1, concat_axis=1, tiled=True),
    )
    resident = jnp.concatenate([resident_pos.reshape(2, -1), resident_strength.reshape(1, -1)])
    settled = resident.at[:, arrived_at.reshape(-1)].set(arrived.reshape(3, -1), mode="drop")
    return fields(settled.reshape(3, half_slots, cells_y, cells_x))


def solution(mesh):
    return jax.shard_map(
        local,
        mesh=mesh,
        in_specs=(
            P(None, "rep", "level", "cell"),
            P("rep", "level", "cell"),
            P(None, "rep", "level", "cell"),
            P("rep", "level", "cell"),
            P("rep", "level", "cell"),
            P("rep", "level", "cell"),
            P("rep", "level", "cell"),
        ),
        out_specs=P(None, "rep", "level", "cell"),
        check_vma=False,
    )
```

time: 1270 us -> 283 us (0.22); the launches traced: 1250 us -> 282 us
  local copies, waits for them, and re-layouts: 763 us -> 148 us
  blocking collectives: 191 us -> 0 us
  matrix products: 96.1 us -> 0 us
  other arithmetic: 82.5 us -> 14.2 us
  Pallas kernels: 0 us -> 68 us
  starting transfers between devices: 71 us -> 35.9 us
  loops' own time: 23 us -> 0 us
  between operations: 17.8 us -> 0.18 us
    slice x371 -> x1, local copies, waits for them, and re-layouts: 423 us -> 0.46 us  [the longest x305 335 us: grouped_far(): padded[:, first_y:first_y + cells_y:2, first_x:first_x + cells_x:2]]
    all_gather x1 -> x0, blocking collectives: 191 us -> none  [local(): lax.all_gather(coarse_own[None], ('cell', 'level'), axis=0, tiled=True)]
    dot_general x96 -> x0, matrix products: 89.4 us -> none  [apply_matrix(): jnp.einsum('ij,jyx->iyx', jnp.asarray(matrix, dtype=jnp.float32), level_f...]
    concatenate x28 -> x0, local copies, waits for them, and re-layouts: 77.2 us -> none  [grouped_far(): jnp.concatenate(pieces, axis=0)]
    pallas_call x0 -> x4, Pallas kernels: none -> 68 us  [the longest x1 45.3 us: fields(): pl.pallas_call(near_kernel, out_shape=shape(2, 16, 32, LANES), scratch_sh...]
    ppermute x20 -> x5, starting transfers between devices: 55.8 us -> 8.8 us  [the longest x4 8.54 us: neighbours(): lax.ppermute(value, axis, [(i, i + step) for i in range(size) if 0 <= i +...]
    unnamed x315 -> x18, local copies, waits for them, and re-layouts: 80.3 us -> 36.1 us
    reduce_sum x11 -> x0, other arithmetic: 41.4 us -> none  [the longest x8 36.7 us: near_band(): real_sum = real_sum + jnp.sum(weight * gap_x, axis=1)]
  transfers between devices with their start and end apart: 23 -> 8, of which waited for: 1 -> 4; matrix products, arithmetic and copies ran while one was open for 45% -> 15% of each run, Pallas kernels for 0% -> 16%
where the time goes in v1:
time: 283 us; the launch traced here: 282 us
  local copies, waits for them, and re-layouts  148 us (52%)
  Pallas kernels  68 us (24%)
  starting transfers between devices  35.9 us (13%)
  waiting for transfers between devices  15.7 us (6%)
  other arithmetic  14.2 us (5%)
    scatter x1, local copies, waits for them, and re-layouts, local(): resident.at[:, arrived_at.reshape(-1)]  62.2 us
    pallas_call x1, Pallas kernels, fields(): pl.pallas_call(near_kernel, out_shape=shape(2, 16, 32, LANES), scratch_sh...  45.3 us
    unnamed x18, local copies, waits for them, and re-layouts  36.1 us
    reshape x1, local copies, waits for them, and re-layouts, local(): return fields(settled.reshape(3, half_slots, cells_y, cells_x))  19.5 us
    concatenate x1, local copies, waits for them, and re-layouts, local(): jnp.concatenate([resident_pos.reshape(2, -1), resident_strength.reshape(1...  16 us
    all_to_all x1, starting transfers between devices, fields(): gathered = lax.all_to_all(coarse, ('cell', 'level'), 0, 0, tiled=True)  12 us
    pallas_call x1, Pallas kernels, fields(): pl.pallas_call(far_kernel, grid_spec=pltpu.PrefetchScalarGridSpec(num_sca...  11.7 us
    all_to_all x1, waiting for transfers between devices, local(): lax.all_to_all(outgoing, 'cell', split_axis=1, concat_axis=1, tiled=True)  8.61 us
  transfers between devices with their start and end apart: 8, of which 4 were waited for; matrix products, arithmetic and copies ran while one was open for 15% of the time, Pallas kernels for 16%

profile of v1, /device:TPU:0, one launch (start us, length us, event | category | flops | bytes accessed | tf_op | source)
XLA Modules:
  0.0 281.5 jit_solution(8175838629169846636)
XLA Ops:
  0.7 4.6 %reduce-window.6 = s32[16,32,128]{2,1,0:T(8,128)S(1)} reduce-window(s32[16,32,128]{2,1,0:T(8,128)S(1)} %fusion.4, s32[]{:T(128)} %constant.25.clone.1), window={size=1x1x128 pad=0_0x0_0x127_0}, to_apply=%region_0.0 | reduce-window | flops 8323072 | bytes 524292 | tf_op jit(solution)/shard_map/reduce-window
  6.2 0.9 fusion.3
  8.6 0.8 and_reduce_fusion.1
  10.2 16.1 %scatter_custom_fusion.1 = s32[16384]{0:T(1024)} fusion(s32[4096]{0:T(1024)S(1)} %broadcast_select_fusion.1, s32[4096]{0:T(1024)S(1)} %bitcast.73, s32[]{:T(128)} %constant.24.clone.1), kind=kCustom, calls=%fused_computation.29 | custom fusion | bytes 65540
  26.3 8.0 %all-to-all-start = ((s32[1,16,1024]{2,0,1:T(1,128)}), s32[1,16,1024]{2,0,1:T(1,128)S(1)}, u32[]{:S(2)}, u32[]{:S(2)}) async-start(s32[1,16,1024]{2,0,1:T(1,128)} %bitcast.10), calls=%async_computation | async-start | bytes 131072 | tf_op jit(solution)/shard_map/all_to_all | solution.py:584
  34.3 0.8 multiply_reduce_fusion.1
  35.0 0.8 and_reduce_fusion
  35.8 0.8 copy.45
  36.6 1.4 copy.44
  38.8 1.4 pad_maximum_fusion
  40.9 14.3 %scatter_custom_fusion.2 = f32[3,16384]{0,1:T(8,128)} fusion(s32[4096]{0:T(1024)S(1)} %broadcast_select_fusion, f32[4096,3]{1,0:T(8,128)S(1)} %copy.31, f32[]{:T(128)} %constant.56.clone.1), kind=kCustom, calls=%fused_computation.3 | custom fusion | bytes 196612
  55.2 5.9 %copy.32 = f32[3,16,1024]{2,0,1:T(4,128)} copy(f32[3,16,1024]{0,2,1:T(8,128)} %bitcast.56) | data formatting | bytes 393216 | tf_op jit(solution)/shard_map/scatter | solution.py:575
  61.1 16.0 %copy.33 = f32[3,65536]{0,1:T(8,128)} copy(f32[3,65536]{1,0:T(4,128)S(1)} %pad_maximum_fusion) | data formatting | bytes 1572864 | tf_op jit(solution)/shard_map/concatenate | solution.py:586
  77.1 7.2 %all-to-all-start.1 = ((f32[3,16,1024]{2,0,1:T(4,128)}), f32[3,16,1024]{2,0,1:T(4,128)S(1)}, u32[]{:S(2)}, u32[]{:S(2)}) async-start(f32[3,16,1024]{2,0,1:T(4,128)} %copy.32), calls=%async_computation.1 | async-start | bytes 524288 | tf_op jit(solution)/shard_map/all_to_all | solution.py:583
  84.4 8.6 %all-to-all-done.1 = f32[3,16,1024]{2,0,1:T(4,128)S(1)} async-done(((f32[3,16,1024]{2,0,1:T(4,128)}), f32[3,16,1024]{2,0,1:T(4,128)S(1)}, u32[]{:S(2)}, u32[]{:S(2)}) %all-to-all-start.1) | async-done | bytes 196640 | tf_op jit(solution)/shard_map/all_to_all | solution.py:583
  93.0 5.0 %copy.34 = f32[16384,3]{1,0:T(8,128)} copy(f32[16384,3]{0,1:T(4,128)S(1)} %bitcast.58) | data formatting | bytes 393216 | tf_op jit(solution)/shard_map/reshape | solution.py:587
  98.0 62.2 %scatter_fusion = f32[3,65536]{0,1:T(8,128)} fusion(f32[3,65536]{0,1:T(8,128)} %copy.33, s32[16384]{0:T(1024)S(1)} %bitcast.61, f32[16384,3]{1,0:T(8,128)} %copy.34), kind=kCustom, calls=%fused_computation | custom fusion | bytes 655360 | tf_op jit(solution)/shard_map/scatter | solution.py:587
  160.2 19.5 %copy.37.own = f32[3,16,32,128]{3,2,1,0:T(8,128)S(1)} copy(f32[3,16,32,128]{0,3,2,1:T(8,128)} %bitcast.55) | data formatting | bytes 1572864 | tf_op jit(solution)/shard_map/reshape | solution.py:588
  180.0 2.3 collective-permute-done.other
  182.3 0.9 copy-done.1
  183.2 7.9 %upward.1 = (f32[2480,128]{1,0:T(8,128)}, f32[2,112,128]{2,1,0:T(8,128)}, f32[64,128]{1,0:T(8,128)}) custom-call(f32[3,16,32,128]{3,2,1,0:T(8,128)} %copy-done, f32[3,16,32,128]{3,2,1,0:T(8,128)} %copy-done.1, bf16[256,128]{1,0:T(8,128)(2,1)} %constant.57.clone.split_ref, bf16[32,240]{1,0:T(8,128)(2,1)} %constant.58.clone.lift_ref, ...), custom_call_target="tpu_custom_call" | custom-call | tf_op jit(solution)/shard_map/upward/pallas_call | solution.py:493
  191.0 0.9 slice_bitcast_fusion.2
  191.9 2.5 collective-permute-start.1
  194.4 1.3 collective-permute-start.2
  196.2 4.3 %collective-permute-done.2.from_right = f32[112,128]{1,0:T(8,128)S(1)} collective-permute-done((f32[112,128]{1,0:T(8,128)S(1)}, f32[112,128]{1,0:T(8,128)S(1)}, u32[]{:S(2)}, u32[]{:S(2)}) %collective-permute-start.2) | collective-permute-done | bytes 57376 | tf_op jit(solution)/shard_map/ppermute | solution.py:485
  201.0 3.1 %rows.1 = f32[2,264,128]{2,1,0:T(8,128)} custom-call(f32[3,16,32,128]{3,2,1,0:T(8,128)} %copy-done, f32[3,16,32,128]{3,2,1,0:T(8,128)} %copy-done.1, f32[2480,128]{1,0:T(8,128)} %get-tuple-element.9.cells, f32[112,128]{1,0:T(8,128)} %copy-done.4, f32[112,128]{1,0:T(8,128)} %copy-done.5), custom_call_target="tpu_custom_call" | custom-call | tf_op jit(solution)/shard_map/rows/pallas_call | solution.py:503
  204.2 1.0 slice_bitcast_fusion
  205.1 3.5 %collective-permute-start.3 = (f32[264,128]{1,0:T(8,128)S(1)}, f32[264,128]{1,0:T(8,128)S(1)}, u32[]{:S(2)}, u32[]{:S(2)}) collective-permute-start(f32[264,128]{1,0:T(8,128)S(1)} %get-tuple-element.12), channel_id=1, source_target_pairs={{0,2},{2,4},{4,6},{1,3},{3,5},{5,7},{8,10},{10,12},{12,14},{9,11},... | collective-permute-start | bytes 405512 | tf_op jit(solution)/shard_map/ppermute | solution.py:485
  208.6 1.3 collective-permute-start.4
  210.0 12.0 %all-to-all-start.2 = ((f32[64,1,128]{2,1,0:T(1,128)}), f32[64,1,128]{2,1,0:T(1,128)S(1)}, u32[]{:S(2)}, u32[]{:S(2)}) async-start(f32[64,1,128]{2,1,0:T(1,128)} %bitcast.71), calls=%async_computation.2 | async-start | bytes 65536 | tf_op jit(solution)/shard_map/all_to_all | solution.py:502
  223.9 45.3 %near.1 = f32[2,16,32,128]{3,2,1,0:T(8,128)} custom-call(f32[3,16,32,128]{3,2,1,0:T(8,128)} %copy-done, f32[3,16,32,128]{3,2,1,0:T(8,128)} %copy-done.1, f32[112,128]{1,0:T(8,128)} %copy-done.4, f32[112,128]{1,0:T(8,128)} %copy-done.5, f32[264,128]{1,0:T(8,128)} %copy-done.2, f32[264,128]{1,0:T(8,128)} %copy-done.3), custom_call_target="tpu_custom_call" | custom-call | tf_op jit(solution)/shard_map/near/pallas_call | solution.py:511
  269.9 11.7 %far.1 = f32[2,16,32,128]{3,2,1,0:T(8,128)} custom-call(s32[2]{0:T(128)} %pad_add_fusion.2.place, f32[3,16,32,128]{3,2,1,0:T(8,128)} %copy-done, f32[2,16,32,128]{3,2,1,0:T(8,128)} %near.1, f32[2480,128]{1,0:T(8,128)} %get-tuple-element.9.cells, f32[112,128]{1,0:T(8,128)} %copy-done.4, f32[112,128]{1,0:T(8,128)} %copy-done.5, f32[264,128]{1,0:T(8,128)} %copy-done.2, ...), custom_call_target="tpu_custom_call" | custom-call | tf_op jit(solution)/shard_map/far/pallas_call | solution.py:540
  (34 shorter events, 9.3 us)
Async XLA Ops:
  26.3 50.8 %all-to-all-start = ((s32[1,16,1024]{2,0,1:T(1,128)}), s32[1,16,1024]{2,0,1:T(1,128)S(1)}, u32[]{:S(2)}, u32[]{:S(2)}) async-start(s32[1,16,1024]{2,0,1:T(1,128)} %bitcast.10), calls=%async_computation | async-start | bytes 131072 | tf_op jit(solution)/shard_map/all_to_all | solution.py:584
  77.1 15.9 %all-to-all-start.1 = ((f32[3,16,1024]{2,0,1:T(4,128)}), f32[3,16,1024]{2,0,1:T(4,128)S(1)}, u32[]{:S(2)}, u32[]{:S(2)}) async-start(f32[3,16,1024]{2,0,1:T(4,128)} %copy.32), calls=%async_computation.1 | async-start | bytes 524288 | tf_op jit(solution)/shard_map/all_to_all | solution.py:583
  179.7 2.6 copy-start
  179.7 2.5 collective-permute-start
  182.3 0.9 copy-start.1
  191.9 4.3 %collective-permute-start.1 = (f32[112,128]{1,0:T(8,128)S(1)}, f32[112,128]{1,0:T(8,128)S(1)}, u32[]{:S(2)}, u32[]{:S(2)}) collective-permute-start(f32[112,128]{1,0:T(8,128)S(1)} %get-tuple-element.14), channel_id=1, source_target_pairs={{0,8},{8,16},{16,24},{24,32},{32,40},{40,48},{48,56},{56,64},{64,7... | collective-permute-start | bytes 172040 | tf_op jit(solution)/shard_map/ppermute | solution.py:485
  194.4 6.1 %collective-permute-start.2 = (f32[112,128]{1,0:T(8,128)S(1)}, f32[112,128]{1,0:T(8,128)S(1)}, u32[]{:S(2)}, u32[]{:S(2)}) collective-permute-start(f32[112,128]{1,0:T(8,128)S(1)} %get-tuple-element.13), channel_id=1, source_target_pairs={{8,0},{16,8},{24,16},{32,24},{40,32},{48,40},{56,48},{64,56},{72,6... | collective-permute-start | bytes 172040 | tf_op jit(solution)/shard_map/ppermute | solution.py:485
  196.2 4.3 %copy-start.4 = (f32[112,128]{1,0:T(8,128)}, f32[112,128]{1,0:T(8,128)S(1)}, u32[]{:S(2)}) copy-start(f32[112,128]{1,0:T(8,128)S(1)} %collective-permute-done.1.from_left) | copy-start | bytes 172036
  200.4 0.6 copy-start.5
  205.1 17.4 %collective-permute-start.3 = (f32[264,128]{1,0:T(8,128)S(1)}, f32[264,128]{1,0:T(8,128)S(1)}, u32[]{:S(2)}, u32[]{:S(2)}) collective-permute-start(f32[264,128]{1,0:T(8,128)S(1)} %get-tuple-element.12), channel_id=1, source_target_pairs={{0,2},{2,4},{4,6},{1,3},{3,5},{5,7},{8,10},{10,12},{12,14},{9,11},... | collective-permute-start | bytes 405512 | tf_op jit(solution)/shard_map/ppermute | solution.py:485
  208.6 14.0 %collective-permute-start.4 = (f32[264,128]{1,0:T(8,128)S(1)}, f32[264,128]{1,0:T(8,128)S(1)}, u32[]{:S(2)}, u32[]{:S(2)}) collective-permute-start(f32[264,128]{1,0:T(8,128)S(1)} %get-tuple-element.11), channel_id=1, source_target_pairs={{2,0},{4,2},{6,4},{3,1},{5,3},{7,5},{10,8},{12,10},{14,12},{11,9},... | collective-permute-start | bytes 405512 | tf_op jit(solution)/shard_map/ppermute | solution.py:485
  210.0 59.3 %all-to-all-start.2 = ((f32[64,1,128]{2,1,0:T(1,128)}), f32[64,1,128]{2,1,0:T(1,128)S(1)}, u32[]{:S(2)}, u32[]{:S(2)}) async-start(f32[64,1,128]{2,1,0:T(1,128)} %bitcast.71), calls=%async_computation.2 | async-start | bytes 65536 | tf_op jit(solution)/shard_map/all_to_all | solution.py:502
  222.6 0.7 copy-start.2
  223.3 0.6 copy-start.3
  269.2 0.6 copy-start.6

commit v2 on v1

--- a/solution.py
+++ b/solution.py
@@ -559,33 +559,160 @@
     )(place, *operands)
 
 
+def flat_index(shape_):
+    rows = lax.broadcasted_iota(jnp.int32, shape_, 0)
+    return rows * LANES + lax.broadcasted_iota(jnp.int32, shape_, 1)
+
+
+def exchange(key, loads, index, distance, descending):
+    high = (index & distance) != 0
+    axis = 1 if distance < LANES else 0
+    step = distance if axis else distance // LANES
+    size = key.shape[axis]
+
+    def partner(value):
+        down = pltpu.roll(value, step, axis)
+        if 2 * step == size:
+            return down
+        return jnp.where(high, down, pltpu.roll(value, size - step, axis))
+
+    flip = high if descending is None else high ^ descending
+    other = partner(key)
+    take = (other < key) ^ flip
+    return jnp.where(take, other, key), [jnp.where(take, partner(load), load) for load in loads]
+
+
+def pack_kernel(odd_ref, pos, strength, owner_ref, leaf, slot, out, keys, values):
+    odd = odd_ref[0]
+    owner = owner_ref[...]
+    address = slot[...] * 4096 + leaf[...]
+    address = jnp.where(odd == 1, 65535 - address, address)
+    key = owner * 65536 + address
+    loads = [pos[0], pos[1], strength[...]]
+    index = flat_index((32, LANES))
+    for block in range(1, 13):
+        descending = None if block == 12 else (index & (1 << block)) != 0
+        for bit in range(block - 1, -1, -1):
+            key, loads = exchange(key, loads, index, 1 << bit, descending)
+    keys[...] = jnp.full(keys.shape, -1, jnp.int32)
+    keys[pl.ds(8, 32), :] = key
+    for c in range(3):
+        values[c, pl.ds(8, 32), :] = loads[c]
+    lane = lane_index(8)
+    for o in range(16):
+        bound = jnp.where(odd == 1, o + 1, o)
+        start = jnp.sum((owner < bound).astype(jnp.int32)) + jnp.where(odd == 1, 0, 1024)
+        row = start // LANES
+        shift = start % LANES
+        back = jnp.where(shift == 0, 0, LANES - shift)
+
+        def window(ref):
+            upper = pltpu.roll(ref[pl.ds(row, 8), :], back, 1)
+            lower = pltpu.roll(ref[pl.ds(row + 1, 8), :], back, 1)
+            return jnp.where(lane < LANES - shift, upper, lower)
+
+        mine = window(keys)
+        place = mine - o * 65536
+        valid = (place >= 0) & (place < 65536)
+        place = jnp.where(odd == 1, 65535 - place, place)
+        out[o, 3] = jnp.where(valid, place, 65536).astype(f32)
+        for c in range(3):
+            out[o, c] = window(values.at[c])
+
+
+def settle_kernel(arrived, pos, strength, out, marks_a, marks_b, loads_a, loads_b):
+    index = flat_index((LANES, LANES))
+    key = arrived[:, 3].reshape(LANES, LANES)
+    loads = [arrived[:, c].reshape(LANES, LANES) for c in range(3)]
+    for block in range(11, 15):
+        descending = None if block == 14 else (index & (1 << block)) != 0
+        for bit in range(block - 1, -1, -1):
+            key, loads = exchange(key, loads, index, 1 << bit, descending)
+    address = key.astype(jnp.int32)
+    mark = jnp.where(address < 65536, 2 * (address - index) + 1, 0)
+    size = 576
+    for ref in (marks_a, marks_b):
+        ref[...] = jnp.zeros((size, LANES), jnp.int32)
+    marks_a[pl.ds(64, LANES), :] = mark
+    for c in range(3):
+        loads_a[c, pl.ds(64, LANES), :] = loads[c]
+    lane = lane_index(64)
+    marks, values = (marks_a, marks_b), (loads_a, loads_b)
+    for bit in range(15, -1, -1):
+        now, later = marks[bit % 2 == 0], marks[bit % 2]
+        load_now, load_later = values[bit % 2 == 0], values[bit % 2]
+        test = 2 << bit
+        rows = (1 << bit) // LANES
+
+        def step(block, _, now=now, later=later, load_now=load_now, load_later=load_later, test=test, rows=rows, bit=bit):
+            base = pl.multiple_of(block * 64, 64)
+            here = pl.ds(base + 64, 64)
+
+            def source(ref):
+                if rows:
+                    if rows >= 64:
+                        start = pl.multiple_of(jnp.maximum(base + 64 - rows, 0), 8)
+                        return ref[pl.ds(start, 64), :]
+                    return ref[pl.ds(base + 64 - rows, 64), :]
+                near = pltpu.roll(ref[here, :], 1 << bit, 1)
+                before = pltpu.roll(ref[pl.ds(base + 63, 64), :], 1 << bit, 1)
+                return jnp.where(lane < (1 << bit), before, near)
+
+            own = now[here, :]
+            own = jnp.where((own & test) != 0, 0, own)
+            there = source(now)
+            come = (there & test) != 0
+            if rows >= 64:
+                come = come & (base >= rows)
+            later[here, :] = jnp.where(come, there, own)
+            for c in range(3):
+                load_later[c, here, :] = jnp.where(come, source(load_now.at[c]), load_now[c, here, :])
+            return 0
+
+        lax.fori_loop(0, 8, step, 0)
+    for j in range(16):
+        rows = pl.ds(64 + 32 * j, 32)
+        moved = marks_a[rows, :] != 0
+        out[0, j] = jnp.where(moved, loads_a[0, rows, :], pos[0, j])
+        out[1, j] = jnp.where(moved, loads_a[1, rows, :], pos[1, j])
+        out[2, j] = jnp.where(moved, loads_a[2, rows, :], strength[j])
+
+
 def local(
     resident_pos, resident_strength, mover_pos, mover_strength, mover_owner, mover_leaf, mover_slot
 ):
-    cell_count = lax.axis_size("cell")
-    half_slots, cells_y, cells_x = resident_strength.shape
-    leaves = cells_y * cells_x
-    owner_cell = mover_owner.reshape(-1)
-    address = mover_slot.reshape(-1) * leaves + mover_leaf.reshape(-1)
-    peer_ids = jnp.arange(cell_count, dtype=jnp.int32)
-    onehot = (owner_cell[:, None] == peer_ids[None, :]).astype(jnp.int32)
-    rank_in_owner = jnp.sum(jnp.cumsum(onehot, axis=0) * onehot, axis=1) - 1
-    values = jnp.concatenate([mover_pos.reshape(2, -1), mover_strength.reshape(1, -1)])
-    outgoing = (
-        jnp.zeros((3, cell_count, CAP), jnp.float32).at[:, owner_cell, rank_in_owner].set(values)
+    smem = pl.BlockSpec(memory_space=pltpu.SMEM)
+    vmem = pl.BlockSpec(memory_space=pltpu.VMEM)
+    odd = (lax.axis_index("cell") % 2).astype(jnp.int32).reshape(1)
+    outgoing = pl.pallas_call(
+        pack_kernel,
+        in_specs=[smem] + [vmem] * 5,
+        out_shape=shape(16, 4, 8, LANES),
+        scratch_shapes=[pltpu.VMEM((56, LANES), jnp.int32), pltpu.VMEM((3, 56, LANES), f32)],
+        compiler_params=params(),
+        name="pack",
+    )(
+        odd,
+        mover_pos.reshape(2, 32, LANES),
+        mover_strength.reshape(32, LANES),
+        mover_owner.reshape(32, LANES),
+        mover_leaf.reshape(32, LANES),
+        mover_slot.reshape(32, LANES),
     )
-    addresses = (
-        jnp.full((1, cell_count, CAP), half_slots * leaves, jnp.int32)
-        .at[0, owner_cell, rank_in_owner]
-        .set(address)
-    )
-    arrived, arrived_at = (
-        lax.all_to_all(outgoing, "cell", split_axis=1, concat_axis=1, tiled=True),
-        lax.all_to_all(addresses, "cell", split_axis=1, concat_axis=1, tiled=True),
-    )
-    resident = jnp.concatenate([resident_pos.reshape(2, -1), resident_strength.reshape(1, -1)])
-    settled = resident.at[:, arrived_at.reshape(-1)].set(arrived.reshape(3, -1), mode="drop")
-    return fields(settled.reshape(3, half_slots, cells_y, cells_x))
+    arrived = lax.all_to_all(outgoing, "cell", 0, 0, tiled=True)
+    own = pl.pallas_call(
+        settle_kernel,
+        out_shape=shape(3, 16, 32, LANES),
+        scratch_shapes=[
+            pltpu.VMEM((576, LANES), jnp.int32),
+            pltpu.VMEM((576, LANES), jnp.int32),
+            pltpu.VMEM((3, 576, LANES), f32),
+            pltpu.VMEM((3, 576, LANES), f32),
+        ],
+        compiler_params=params(),
+        name="settle",
+    )(arrived, resident_pos, resident_strength)
+    return fields(own)
 
 
 def solution(mesh):

time: 283 us -> 140 us (0.49)
  local copies, waits for them, and re-layouts: 148 us -> 5.26 us
  Pallas kernels: 68 us -> 90.4 us
  blocking collectives: 0 us -> 16.8 us
  starting transfers between devices: 35.9 us -> 21.8 us
  other arithmetic: 14.2 us -> 0.56 us
  waiting for transfers between devices: 15.7 us -> 4.31 us
    scatter x2 -> x0, local copies, waits for them, and re-layouts: 68.1 us -> none  [the longest x1 62.2 us: local(): resident.at[:, arrived_at.reshape(-1)]]
    unnamed x18 -> x12, local copies, waits for them, and re-layouts: 36.1 us -> 3.41 us
    reshape x2 -> x0, local copies, waits for them, and re-layouts: 24.4 us -> none  [the longest x1 19.5 us: local(): return fields(settled.reshape(3, half_slots, cells_y, cells_x))]
    pallas_call x0 -> x2, Pallas kernels: none -> 22.4 us  [the longest x1 15.7 us: local(): pl.pallas_call(settle_kernel, out_shape=shape(3, 16, 32, LANES), scratch_...]
    all_to_all x0 -> x1, blocking collectives: none -> 16.8 us  [local(): arrived = lax.all_to_all(outgoing, 'cell', 0, 0, tiled=True)]
    concatenate x2 -> x0, local copies, waits for them, and re-layouts: 16.7 us -> none  [the longest x1 16 us: local(): jnp.concatenate([resident_pos.reshape(2, -1), resident_strength.reshape(1...]
    all_to_all x2 -> x0, starting transfers between devices: 15.2 us -> none  [the longest x1 7.96 us: local(): lax.all_to_all(addresses, 'cell', split_axis=1, concat_axis=1, tiled=True)]
    all_to_all x2 -> x0, waiting for transfers between devices: 8.62 us -> none  [the longest x1 8.61 us: local(): lax.all_to_all(outgoing, 'cell', split_axis=1, concat_axis=1, tiled=True)]
  transfers between devices with their start and end apart: 8 -> 6, of which waited for: 4 -> 3; matrix products, arithmetic and copies ran while one was open for 15% -> 0% of each run, Pallas kernels for 16% -> 33%
where the time goes in v2:
time: 140 us; the launch traced here: 139 us
  Pallas kernels  90.4 us (65%)
  starting transfers between devices  21.8 us (16%)
  blocking collectives  16.8 us (12%)
  local copies, waits for them, and re-layouts  5.26 us (4%)
  waiting for transfers between devices  4.31 us (3%)
    pallas_call x1, Pallas kernels, fields(): pl.pallas_call(near_kernel, out_shape=shape(2, 16, 32, LANES), scratch_sh...  45.3 us
    all_to_all x1, blocking collectives, local(): arrived = lax.all_to_all(outgoing, 'cell', 0, 0, tiled=True)  16.8 us
    pallas_call x1, Pallas kernels, local(): pl.pallas_call(settle_kernel, out_shape=shape(3, 16, 32, LANES), scratch_...  15.7 us
    ppermute x4, starting transfers between devices, neighbours(): lax.ppermute(value, axis, [(i, i + step) for i in range(size) if 0 <= i +...  11.7 us
    pallas_call x1, Pallas kernels, fields(): pl.pallas_call(far_kernel, grid_spec=pltpu.PrefetchScalarGridSpec(num_sca...  11.7 us
    all_to_all x1, starting transfers between devices, fields(): gathered = lax.all_to_all(coarse, ('cell', 'level'), 0, 0, tiled=True)  10.1 us
    pallas_call x1, Pallas kernels, fields(): pl.pallas_call(upward_kernel, out_shape=(shape(ROWS * FAMILY, LANES), sha...  7.89 us
    pallas_call x1, Pallas kernels, local(): pl.pallas_call(pack_kernel, in_specs=[smem] + [vmem] * 5, out_shape=shape...  6.7 us
  transfers between devices with their start and end apart: 6, of which 3 were waited for; matrix products, arithmetic and copies ran while one was open for 0% of the time, Pallas kernels for 33%

profile of v2, /device:TPU:0, one launch (start us, length us, event | category | flops | bytes accessed | tf_op | source)
XLA Modules:
  0.0 139.1 jit_solution(7648440939307765027)
XLA Ops:
  0.0 6.7 %pack.1 = f32[16,4,8,128]{3,2,1,0:T(8,128)} custom-call(s32[1]{0:T(128)} %bitcast.2.odd_ref, f32[2,32,128]{2,1,0:T(8,128)} %bitcast.21, f32[32,128]{1,0:T(8,128)} %bitcast.22, s32[32,128]{1,0:T(8,128)} %bitcast.23, s32[32,128]{1,0:T(8,128)} %bitcast.24, s32[32,128]{1,0:T(8,128)} %bitcast.25), custom_call_target="tpu_custom_call" | custom-call | tf_op jit(solution)/shard_map/pack/pallas_call | solution.py:687
  6.7 16.8 %all_to_all.16.arrived = f32[16,4,8,128]{3,2,1,0:T(8,128)} all-to-all(f32[16,4,8,128]{3,2,1,0:T(8,128)} %pack.1), channel_id=1, replica_groups=mesh['cell'=16,'level'=4,'rep'=2] {'cell'}, dimensions={0} | all-to-all | bytes 524288 | tf_op jit(solution)/shard_map/all_to_all | solution.py:702
  23.5 15.7 %settle.1.own = f32[3,16,32,128]{3,2,1,0:T(8,128)} custom-call(f32[16,4,8,128]{3,2,1,0:T(8,128)} %all_to_all.16.arrived, f32[2,16,32,128]{3,2,1,0:T(8,128)} %pos.1, f32[16,32,128]{2,1,0:T(8,128)} %strength.1), custom_call_target="tpu_custom_call" | custom-call | tf_op jit(solution)/shard_map/settle/pallas_call | solution.py:703
  39.1 0.0 collective-permute-start
  39.1 2.5 %collective-permute-done.other = f32[3,16,32,128]{3,2,1,0:T(8,128)S(1)} collective-permute-done((f32[3,16,32,128]{3,2,1,0:T(8,128)}, f32[3,16,32,128]{3,2,1,0:T(8,128)S(1)}, u32[]{:S(2)}, u32[]{:S(2)}) %collective-permute-start) | collective-permute-done | bytes 786464 | tf_op jit(solution)/shard_map/ppermute | solution.py:489
  41.6 0.0 copy-start
  41.6 0.9 copy-done
  42.5 7.9 %upward.1 = (f32[2480,128]{1,0:T(8,128)}, f32[2,112,128]{2,1,0:T(8,128)}, f32[64,128]{1,0:T(8,128)}) custom-call(f32[3,16,32,128]{3,2,1,0:T(8,128)} %settle.1.own, f32[3,16,32,128]{3,2,1,0:T(8,128)} %copy-done, bf16[256,128]{1,0:T(8,128)(2,1)} %constant.46.clone.split_ref, bf16[32,240]{1,0:T(8,128)(2,1)} %constant.47.clone.lift_ref, ...), custom_call_target="tpu_custom_call" | custom-call | tf_op jit(solution)/shard_map/upward/pallas_call | solution.py:493
  50.4 0.9 slice_bitcast_fusion.2
  51.3 1.3 collective-permute-start.2
  52.6 4.5 %collective-permute-start.1 = (f32[112,128]{1,0:T(8,128)S(1)}, f32[112,128]{1,0:T(8,128)S(1)}, u32[]{:S(2)}, u32[]{:S(2)}) collective-permute-start(f32[112,128]{1,0:T(8,128)S(1)} %get-tuple-element.14), channel_id=1, source_target_pairs={{0,8},{8,16},{16,24},{24,32},{32,40},{40,48},{48,56},{56,64},{64,7... | collective-permute-start | bytes 172040 | tf_op jit(solution)/shard_map/ppermute | solution.py:485
  57.1 0.2 collective-permute-done.2.from_right
  57.3 0.0 copy-start.3
  57.3 1.6 %collective-permute-done.1.from_left = f32[112,128]{1,0:T(8,128)S(1)} collective-permute-done((f32[112,128]{1,0:T(8,128)S(1)}, f32[112,128]{1,0:T(8,128)S(1)}, u32[]{:S(2)}, u32[]{:S(2)}) %collective-permute-start.1) | collective-permute-done | bytes 57376 | tf_op jit(solution)/shard_map/ppermute | solution.py:485
  58.9 0.0 copy-start.4
  58.9 0.0 copy-done.3
  58.9 0.6 copy-done.4
  59.6 3.1 %rows.1 = f32[2,264,128]{2,1,0:T(8,128)} custom-call(f32[3,16,32,128]{3,2,1,0:T(8,128)} %settle.1.own, f32[3,16,32,128]{3,2,1,0:T(8,128)} %copy-done, f32[2480,128]{1,0:T(8,128)} %get-tuple-element.9.cells, f32[112,128]{1,0:T(8,128)} %copy-done.4, f32[112,128]{1,0:T(8,128)} %copy-done.3), custom_call_target="tpu_custom_call" | custom-call | tf_op jit(solution)/shard_map/rows/pallas_call | solution.py:503
  62.7 1.0 slice_bitcast_fusion
  63.7 1.3 collective-permute-start.4
  65.0 4.6 %collective-permute-start.3 = (f32[264,128]{1,0:T(8,128)S(1)}, f32[264,128]{1,0:T(8,128)S(1)}, u32[]{:S(2)}, u32[]{:S(2)}) collective-permute-start(f32[264,128]{1,0:T(8,128)S(1)} %get-tuple-element.12), channel_id=1, source_target_pairs={{0,2},{2,4},{4,6},{1,3},{3,5},{5,7},{8,10},{10,12},{12,14},{9,11},... | collective-permute-start | bytes 405512 | tf_op jit(solution)/shard_map/ppermute | solution.py:485
  69.5 10.1 %all-to-all-start.1 = ((f32[64,1,128]{2,1,0:T(1,128)}), f32[64,1,128]{2,1,0:T(1,128)S(1)}, u32[]{:S(2)}, u32[]{:S(2)}) async-start(f32[64,1,128]{2,1,0:T(1,128)} %bitcast.13), calls=%async_computation.1 | async-start | bytes 65536 | tf_op jit(solution)/shard_map/all_to_all | solution.py:502
  79.6 0.6 pad_add_fusion.place
  80.2 0.0 collective-permute-done.4.below
  80.2 0.0 copy-start.1
  80.2 0.0 collective-permute-done.3.above
  80.2 0.7 copy-done.1
  80.9 0.6 copy-done.2
  81.5 45.3 %near.1 = f32[2,16,32,128]{3,2,1,0:T(8,128)} custom-call(f32[3,16,32,128]{3,2,1,0:T(8,128)} %settle.1.own, f32[3,16,32,128]{3,2,1,0:T(8,128)} %copy-done, f32[112,128]{1,0:T(8,128)} %copy-done.4, f32[112,128]{1,0:T(8,128)} %copy-done.3, f32[264,128]{1,0:T(8,128)} %copy-done.2, f32[264,128]{1,0:T(8,128)} %copy-done.1), custom_call_target="tpu_custom_call" | custom-call | tf_op jit(solution)/shard_map/near/pallas_call | solution.py:511
  126.8 0.0 all-to-all-done.1
  126.8 0.6 copy-done.5
  127.4 11.7 %far.1 = f32[2,16,32,128]{3,2,1,0:T(8,128)} custom-call(s32[2]{0:T(128)} %pad_add_fusion.place, f32[3,16,32,128]{3,2,1,0:T(8,128)} %settle.1.own, f32[2,16,32,128]{3,2,1,0:T(8,128)} %near.1, f32[2480,128]{1,0:T(8,128)} %get-tuple-element.9.cells, f32[112,128]{1,0:T(8,128)} %copy-done.4, f32[112,128]{1,0:T(8,128)} %copy-done.3, f32[264,128]{1,0:T(8,128)} %copy-done.2, ...), custom_call_target="tpu_custom_call" | custom-call | tf_op jit(solution)/shard_map/far/pallas_call | solution.py:540
  (2 shorter events, 0.0 us)
Async XLA Ops:
  39.1 2.5 %collective-permute-start = (f32[3,16,32,128]{3,2,1,0:T(8,128)}, f32[3,16,32,128]{3,2,1,0:T(8,128)S(1)}, u32[]{:S(2)}, u32[]{:S(2)}) collective-permute-start(f32[3,16,32,128]{3,2,1,0:T(8,128)} %settle.1.own), channel_id=1, source_target_pairs={{0,1},{1,0},{2,3},{3,2},{4,5},{5,4},{6,7},{7,6},{8,9},{9,8},{10,11... | collective-permute-start | bytes 2359304 | tf_op jit(solution)/shard_map/ppermute | solution.py:489
  41.6 0.9 copy-start
  51.3 6.1 %collective-permute-start.2 = (f32[112,128]{1,0:T(8,128)S(1)}, f32[112,128]{1,0:T(8,128)S(1)}, u32[]{:S(2)}, u32[]{:S(2)}) collective-permute-start(f32[112,128]{1,0:T(8,128)S(1)} %get-tuple-element.13), channel_id=1, source_target_pairs={{8,0},{16,8},{24,16},{32,24},{40,32},{48,40},{56,48},{64,56},{72,6... | collective-permute-start | bytes 172040 | tf_op jit(solution)/shard_map/ppermute | solution.py:485
  52.6 6.4 %collective-permute-start.1 = (f32[112,128]{1,0:T(8,128)S(1)}, f32[112,128]{1,0:T(8,128)S(1)}, u32[]{:S(2)}, u32[]{:S(2)}) collective-permute-start(f32[112,128]{1,0:T(8,128)S(1)} %get-tuple-element.14), channel_id=1, source_target_pairs={{0,8},{8,16},{16,24},{24,32},{32,40},{40,48},{48,56},{56,64},{64,7... | collective-permute-start | bytes 172040 | tf_op jit(solution)/shard_map/ppermute | solution.py:485
  57.3 1.6 %copy-start.3 = (f32[112,128]{1,0:T(8,128)}, f32[112,128]{1,0:T(8,128)S(1)}, u32[]{:S(2)}) copy-start(f32[112,128]{1,0:T(8,128)S(1)} %collective-permute-done.2.from_right) | copy-start | bytes 172036
  58.9 0.6 copy-start.4
  63.7 16.5 %collective-permute-start.4 = (f32[264,128]{1,0:T(8,128)S(1)}, f32[264,128]{1,0:T(8,128)S(1)}, u32[]{:S(2)}, u32[]{:S(2)}) collective-permute-start(f32[264,128]{1,0:T(8,128)S(1)} %get-tuple-element.11), channel_id=1, source_target_pairs={{2,0},{4,2},{6,4},{3,1},{5,3},{7,5},{10,8},{12,10},{14,12},{11,9},... | collective-permute-start | bytes 405512 | tf_op jit(solution)/shard_map/ppermute | solution.py:485
  65.0 15.2 %collective-permute-start.3 = (f32[264,128]{1,0:T(8,128)S(1)}, f32[264,128]{1,0:T(8,128)S(1)}, u32[]{:S(2)}, u32[]{:S(2)}) collective-permute-start(f32[264,128]{1,0:T(8,128)S(1)} %get-tuple-element.12), channel_id=1, source_target_pairs={{0,2},{2,4},{4,6},{1,3},{3,5},{5,7},{8,10},{10,12},{12,14},{9,11},... | collective-permute-start | bytes 405512 | tf_op jit(solution)/shard_map/ppermute | solution.py:485
  69.5 57.3 %all-to-all-start.1 = ((f32[64,1,128]{2,1,0:T(1,128)}), f32[64,1,128]{2,1,0:T(1,128)S(1)}, u32[]{:S(2)}, u32[]{:S(2)}) async-start(f32[64,1,128]{2,1,0:T(1,128)} %bitcast.13), calls=%async_computation.1 | async-start | bytes 65536 | tf_op jit(solution)/shard_map/all_to_all | solution.py:502
  80.2 0.7 copy-start.1
  80.9 0.6 copy-start.2
  126.8 0.6 copy-start.5

commit v3 on v2

--- a/solution.py
+++ b/solution.py
@@ -245,18 +245,14 @@
 
     lane32 = lane_index(32)
 
-    def edge(j, sides):
-        left, right = sides
-        for half, ref in enumerate((own, other)):
-            for comp in range(3):
+    left = right = jnp.zeros((32, LANES), f32)
+    for half, ref in enumerate((own, other)):
+        for comp in range(3):
+            for j in range(16):
                 m = comp * 32 + half * 16 + j
                 value = ref[comp, j]
                 left = jnp.where(lane32 == m, pltpu.roll(value, m, 1), left)
                 right = jnp.where(lane32 == m, pltpu.roll(value, m + 1, 1), right)
-        return left, right
-
-    zero = jnp.zeros((32, LANES), f32)
-    left, right = lax.fori_loop(0, 16, edge, (zero, zero))
     packed[0, pl.ds(0, 32), :] = left
     packed[1, pl.ds(0, 32), :] = right
 
@@ -267,8 +263,10 @@
     return jnp.where(lane == width, pltpu.roll(from_right, (width - index) % LANES, 1), parent)
 
 
-def rows_kernel(own, other, cells, from_left, from_right, out):
+def rows_kernel(place, own, other, cells, came_left, came_right, out, from_left, from_right):
     lane80 = lane_index(FAMILY)
+    from_left[...] = jnp.where(place[0] > 0, came_left[...], 0.0)
+    from_right[...] = jnp.where(place[0] < 15, came_right[...], 0.0)
     left, right = from_left[pl.ds(32, FAMILY), :], from_right[pl.ds(32, FAMILY), :]
     for side in (0, 1):
         row = 31 * side
@@ -296,41 +294,35 @@
 GROUP = 8
 
 
-def near_kernel(own, other, from_left, from_right, above, below, out, src):
+def near_kernel(place, own, other, from_left, from_right, came_above, came_below, out, src, above, below):
+    above[...] = jnp.where(place[1] > 0, came_above[pl.ds(0, 104), :], 0.0)
+    below[...] = jnp.where(place[1] < 3, came_below[pl.ds(0, 104), :], 0.0)
     lane32 = lane_index(32)
     lane1 = lane_index(1)
 
     for comp in range(3):
         for half, ref in enumerate((own, other)):
-
-            def frame(j, _, comp=comp, half=half, ref=ref):
+            for j in range(16):
                 m = comp * 32 + half * 16 + j
-                back = (LANES - m) % LANES if isinstance(m, int) else LANES - m
-                value = ref[comp, j]
-                rows = (value, above[pl.ds(m, 1), :], below[pl.ds(m, 1), :])
+                rows = (ref[comp, j], above[pl.ds(m, 1), :], below[pl.ds(m, 1), :])
                 lefts = (from_left[pl.ds(0, 32), :], above[pl.ds(96, 1), :], below[pl.ds(96, 1), :])
                 rights = (from_right[pl.ds(0, 32), :], above[pl.ds(97, 1), :], below[pl.ds(97, 1), :])
                 for part in range(3):
                     place = (pl.ds(8, 32), pl.ds(7, 1), pl.ds(40, 1))[part]
                     lane = lane32 if part == 0 else lane1
                     middle = rows[part]
-                    before = jnp.where(
-                        lane == 0, pltpu.roll(lefts[part], back, 1), pltpu.roll(middle, 1, 1)
-                    )
-                    after = jnp.where(
-                        lane == LANES - 1,
-                        pltpu.roll(rights[part], LANES - 1 - m, 1),
-                        pltpu.roll(middle, LANES - 1, 1),
-                    )
+                    before = pltpu.roll(middle, 1, 1)
+                    after = pltpu.roll(middle, LANES - 1, 1)
+                    left = pltpu.roll(lefts[part], (LANES - m) % LANES, 1)
+                    right = pltpu.roll(rights[part], (LANES - 1 - m) % LANES, 1)
+                    before = jnp.where(lane == 0, left, before)
+                    after = jnp.where(lane == LANES - 1, right, after)
                     if comp == 0:
                         before = before - 1.0
                         after = after + 1.0
                     src[0, m, place, :] = before
                     src[1, m, place, :] = middle
                     src[2, m, place, :] = after
-                return 0
-
-            lax.fori_loop(0, 16, frame, 0)
 
     for tile in range(4):
         for group in range(16 // GROUP):
@@ -353,10 +345,34 @@
                             acc[GROUP + i] = acc[GROUP + i] + weight * gap_y
                         return tuple(acc)
 
-                    acc = lax.fori_loop(0, 32, pairs, acc, unroll=4)
+                    acc = lax.fori_loop(0, 32, pairs, acc, unroll=8)
             for i in range(GROUP):
                 out[0, group * GROUP + i, pl.ds(8 * tile, 8), :] = acc[i]
                 out[1, group * GROUP + i, pl.ds(8 * tile, 8), :] = acc[GROUP + i]
+
+
+def three_products(value, table):
+    product = dot(jnp.concatenate(halves(value), axis=0), table)
+    return product[:16, :LANES] + product[16:, :LANES] + product[:16, LANES:]
+
+
+def packed_parts(value):
+    high = value.astype(bf16).astype(f32)
+    low = value - high
+    return (high + pltpu.roll(low, 32, 1) + pltpu.roll(high, 64, 1)).astype(bf16)
+
+
+def side_by_side(table):
+    return np.concatenate(halves_np(table), axis=-1)
+
+
+def packed_table(table):
+    high, low = halves_np(table)
+    out = np.zeros(table.shape, jnp.bfloat16)
+    out[..., 0:32, :] = high[..., 0:32, :]
+    out[..., 32:64, :] = high[..., 0:32, :]
+    out[..., 64:96, :] = low[..., 0:32, :]
+    return out
 
 
 def far_kernel(
@@ -366,33 +382,38 @@
 ):
     cell = place[0]
     level = place[1]
-    tops = jnp.zeros((16, LANES), f32)
-    for row in range(4):
-        tops = tops + jnp.dot(gathered[pl.ds(row, 16, stride=4), :], to_top[row], precision=precise)
-    spread = jnp.dot(tops, top_ref[...], precision=precise)
+    tops = three_products(
+        jnp.concatenate([gathered[pl.ds(row, 16, stride=4), :] for row in range(4)], axis=1), to_top[...]
+    )
+    spread = dot(packed_parts(tops), top_ref[...])
     source = lax.broadcasted_iota(jnp.int32, (16, 1024), 0)
     step = lax.broadcasted_iota(jnp.int32, (16, 1024), 1) // 32
     line = jnp.sum(jnp.where(step == source - cell + 15, spread, 0.0), axis=0, keepdims=True)
     total = line[:, :LANES]
     for block in range(1, 8):
         total = total + line[:, LANES * block : LANES * (block + 1)]
-    total = jnp.broadcast_to(total, (8, LANES))
+    total = jnp.broadcast_to(total, (16, LANES))
     total = total + pltpu.roll(total, 64, 1)
     total = total + pltpu.roll(total, 32, 1)
-    total = jnp.where(lane_index(8) < CHAN, total, 0.0)
-    five = jnp.dot(total, from_top[0], precision=precise)
+    total = jnp.where(lane_index(16) < CHAN, total, 0.0)
+    around = []
     for step in range(3):
         there = cell + step - 1
-        valid = jnp.where((there >= 0) & (there < 16), 1.0, 0.0)
+        inside = (there >= 0) & (there < 16)
         there = jnp.clip(there, 0, 15)
         for row in range(4):
-            value = jnp.broadcast_to(gathered[pl.ds(there * 4 + row, 1), :], (8, LANES)) * valid
-            five = five + jnp.dot(value, near5[0, step * 4 + row], precision=precise)
+            value = gathered[pl.ds(there * 4 + row, 1), :]
+            around.append(jnp.broadcast_to(jnp.where(inside, value, 0.0), (16, LANES)))
+    five = dot(packed_parts(total), from_top[0]) + three_products(
+        jnp.concatenate(around, axis=1), near5[0]
+    )
     five = jnp.broadcast_to(five[0:1], (32, LANES))
     row32 = lax.broadcasted_iota(jnp.int32, (32, LANES), 0)
     five = jnp.where((lane_index(32) // 4 == row32) & (row32 < CHAN), five, 0.0)
     loc[...] = jnp.zeros(loc.shape, f32)
-    loc[pl.ds(0, 32), pl.ds(0, LANES)] = jnp.dot(five, spread_ref[...], precision=precise)
+    loc[pl.ds(0, 32), pl.ds(0, LANES)] = dot(
+        jnp.concatenate(halves(five), axis=1), spread_ref[...]
+    )
 
     lane80 = lane_index(FAMILY)
     left, right = from_left[pl.ds(32, FAMILY), :], from_right[pl.ds(32, FAMILY), :]
@@ -403,6 +424,7 @@
         for row in range(-1, height + 1):
             if row in (-1, height):
                 ref = above if row == -1 else below
+                inside = level > 0 if row == -1 else level < 3
                 if k == 0:
                     parent = ref[pl.ds(104, FAMILY), :]
                 else:
@@ -413,6 +435,8 @@
                 index = OFFSETS[k] + row
                 parent = cells[pl.ds(FAMILY * index, FAMILY), :]
                 parent = ring_columns(parent, k, index, left, right, lane80)
+            if row in (-1, height):
+                parent = jnp.where(inside, parent, 0.0)
             part_high, part_low = halves(parent)
             high[pl.ds(FAMILY * start, FAMILY), :] = part_high
             low[pl.ds(FAMILY * start, FAMILY), :] = part_low
@@ -482,10 +506,12 @@
 
 def neighbours(value, axis, step):
     size = lax.axis_size(axis)
-    return lax.ppermute(value, axis, [(i, i + step) for i in range(size) if 0 <= i + step < size])
-
-
-def fields(own):
+    return lax.ppermute(value, axis, [(i, (i + step) % size) for i in range(size)])
+
+
+def fields(own, place):
+    smem = pl.BlockSpec(memory_space=pltpu.SMEM)
+    vmem = pl.BlockSpec(memory_space=pltpu.VMEM)
     other = lax.ppermute(own, "rep", [(0, 1), (1, 0)])
     lift_high, lift_low = halves_np(upward_family())
     lift = np.zeros((32, 3 * FAMILY), jnp.bfloat16)
@@ -500,21 +526,28 @@
     from_left = neighbours(packed[1], "cell", 1)
     from_right = neighbours(packed[0], "cell", -1)
     gathered = lax.all_to_all(coarse, ("cell", "level"), 0, 0, tiled=True)
-    rows = pl.pallas_call(
+    sides = shape(32 + FAMILY, LANES)
+    rows, from_left, from_right = pl.pallas_call(
         rows_kernel,
-        out_shape=shape(2, 104 + 2 * FAMILY, LANES),
+        in_specs=[smem] + [vmem] * 5,
+        out_shape=(shape(2, 104 + 2 * FAMILY, LANES), sides, sides),
         compiler_params=params(),
         name="rows",
-    )(own, other, cells, from_left, from_right)
+    )(place, own, other, cells, from_left, from_right)
     above = neighbours(rows[1], "level", 1)
     below = neighbours(rows[0], "level", -1)
     near = pl.pallas_call(
         near_kernel,
+        in_specs=[smem] + [vmem] * 6,
         out_shape=shape(2, 16, 32, LANES),
-        scratch_shapes=[pltpu.VMEM((3, 96, 48, LANES), f32)],
+        scratch_shapes=[
+            pltpu.VMEM((3, 96, 48, LANES), f32),
+            pltpu.VMEM((104, LANES), f32),
+            pltpu.VMEM((104, LANES), f32),
+        ],
         compiler_params=params(),
         name="near",
-    )(own, other, from_left, from_right, above, below)
+    )(place, own, other, from_left, from_right, above, below)
     far_high, far_low = halves_np(far_family())
     drop_table = np.zeros((FAMILY, 32))
     drop_table[:, :CHAN] = downward_family()
@@ -524,19 +557,18 @@
         np.concatenate([far_high, far_low], axis=0),
         np.concatenate([drop_high, drop_high, drop_low], axis=1),
         join_lanes(),
-        quarter_lanes(),
-        to_top.astype(np.float32),
-        near5.astype(np.float32),
-        from_top.astype(np.float32),
-        top.astype(np.float32),
+        np.concatenate([quarter_lanes()] * 2, axis=0).astype(jnp.bfloat16),
+        side_by_side(to_top.reshape(4 * LANES, LANES)),
+        side_by_side(near5.reshape(4, 12 * LANES, LANES)),
+        packed_table(from_top),
+        packed_table(top),
     ]
     operands = [own, near, cells, from_left, from_right, above, below, gathered] + [
         jnp.asarray(table) for table in tables
     ]
     specs = [whole(value.shape) for value in operands]
-    specs[13] = pl.BlockSpec((1, 12, LANES, LANES), lambda i, place: (place[1], 0, 0, 0))
+    specs[13] = pl.BlockSpec((1, 12 * LANES, 2 * LANES), lambda i, place: (place[1], 0, 0))
     specs[14] = pl.BlockSpec((1, LANES, LANES), lambda i, place: (place[1], 0, 0))
-    place = jnp.stack([lax.axis_index("cell"), lax.axis_index("level")]).astype(jnp.int32)
     return pl.pallas_call(
         far_kernel,
         grid_spec=pltpu.PrefetchScalarGridSpec(
@@ -564,44 +596,75 @@
     return rows * LANES + lax.broadcasted_iota(jnp.int32, shape_, 1)
 
 
-def exchange(key, loads, index, distance, descending):
-    high = (index & distance) != 0
-    axis = 1 if distance < LANES else 0
-    step = distance if axis else distance // LANES
-    size = key.shape[axis]
+def swap_step(arrays, bit, high, descending, lanes):
+    distance = 1 << bit
 
     def partner(value):
-        down = pltpu.roll(value, step, axis)
-        if 2 * step == size:
-            return down
-        return jnp.where(high, down, pltpu.roll(value, size - step, axis))
-
-    flip = high if descending is None else high ^ descending
+        if distance >= LANES:
+            step = distance // LANES
+            down = pltpu.roll(value, step, 0)
+            return down if step == 4 else jnp.where(high, down, pltpu.roll(value, 8 - step, 0))
+        if distance == 64:
+            return pltpu.roll(value, 64, 1)
+        return jnp.take_along_axis(value, lanes ^ distance, axis=1)
+
+    key = arrays[0]
     other = partner(key)
+    flip = high if descending is False else (~high if descending is True else high ^ descending)
     take = (other < key) ^ flip
-    return jnp.where(take, other, key), [jnp.where(take, partner(load), load) for load in loads]
-
-
-def pack_kernel(odd_ref, pos, strength, owner_ref, leaf, slot, out, keys, values):
-    odd = odd_ref[0]
+    return [jnp.where(take, other, key)] + [jnp.where(take, partner(x), x) for x in arrays[1:]]
+
+
+def bitonic(tiles, first_block, last_block):
+    index = flat_index((8, LANES))
+    lanes = lax.broadcasted_iota(jnp.int32, (8, LANES), 1)
+    highs = [(index & (1 << bit)) != 0 for bit in range(10)]
+    count = len(tiles)
+    for block in range(first_block, last_block + 1):
+
+        def descending(v):
+            if block == last_block:
+                return False
+            return bool((v >> (block - 10)) & 1) if block >= 10 else highs[block]
+
+        for bit in range(block - 1, -1, -1):
+            if bit >= 10:
+                step = 1 << (bit - 10)
+                for v in range(count):
+                    if v & step:
+                        continue
+                    low, high = tiles[v], tiles[v + step]
+                    take = high[0] > low[0] if descending(v) else high[0] < low[0]
+                    tiles[v] = [jnp.where(take, y, x) for x, y in zip(low, high)]
+                    tiles[v + step] = [jnp.where(take, x, y) for x, y in zip(low, high)]
+            else:
+                for v in range(count):
+                    tiles[v] = swap_step(tiles[v], bit, highs[bit], descending(v), lanes)
+    return tiles
+
+
+def pack_kernel(place_ref, pos, strength, owner_ref, leaf, slot, out, keys, values):
+    odd = place_ref[0] % 2
     owner = owner_ref[...]
     address = slot[...] * 4096 + leaf[...]
     address = jnp.where(odd == 1, 65535 - address, address)
     key = owner * 65536 + address
-    loads = [pos[0], pos[1], strength[...]]
-    index = flat_index((32, LANES))
-    for block in range(1, 13):
-        descending = None if block == 12 else (index & (1 << block)) != 0
-        for bit in range(block - 1, -1, -1):
-            key, loads = exchange(key, loads, index, 1 << bit, descending)
+    starts = []
+    for o in range(16):
+        bound = jnp.where(odd == 1, o + 1, o)
+        before = (owner < bound).astype(jnp.int32)
+        before = before[0:8] + before[8:16] + before[16:24] + before[24:32]
+        starts.append(jnp.sum(before) + jnp.where(odd == 1, 0, 1024))
+    loads = (key, pos[0], pos[1], strength[...])
+    tiles = bitonic([[load[8 * v : 8 * v + 8] for load in loads] for v in range(4)], 1, 12)
     keys[...] = jnp.full(keys.shape, -1, jnp.int32)
-    keys[pl.ds(8, 32), :] = key
-    for c in range(3):
-        values[c, pl.ds(8, 32), :] = loads[c]
+    for v in range(4):
+        keys[pl.ds(8 + 8 * v, 8), :] = tiles[v][0]
+        for c in range(3):
+            values[c, pl.ds(8 + 8 * v, 8), :] = tiles[v][1 + c]
     lane = lane_index(8)
     for o in range(16):
-        bound = jnp.where(odd == 1, o + 1, o)
-        start = jnp.sum((owner < bound).astype(jnp.int32)) + jnp.where(odd == 1, 0, 1024)
+        start = starts[o]
         row = start // LANES
         shift = start % LANES
         back = jnp.where(shift == 0, 0, LANES - shift)
@@ -621,21 +684,16 @@
 
 
 def settle_kernel(arrived, pos, strength, out, marks_a, marks_b, loads_a, loads_b):
-    index = flat_index((LANES, LANES))
-    key = arrived[:, 3].reshape(LANES, LANES)
-    loads = [arrived[:, c].reshape(LANES, LANES) for c in range(3)]
-    for block in range(11, 15):
-        descending = None if block == 14 else (index & (1 << block)) != 0
-        for bit in range(block - 1, -1, -1):
-            key, loads = exchange(key, loads, index, 1 << bit, descending)
-    address = key.astype(jnp.int32)
-    mark = jnp.where(address < 65536, 2 * (address - index) + 1, 0)
-    size = 576
+    tiles = bitonic([[arrived[v, c] for c in (3, 0, 1, 2)] for v in range(16)], 11, 14)
+    index = flat_index((8, LANES))
     for ref in (marks_a, marks_b):
-        ref[...] = jnp.zeros((size, LANES), jnp.int32)
-    marks_a[pl.ds(64, LANES), :] = mark
-    for c in range(3):
-        loads_a[c, pl.ds(64, LANES), :] = loads[c]
+        ref[...] = jnp.zeros(ref.shape, jnp.int32)
+    for v in range(16):
+        address = tiles[v][0].astype(jnp.int32)
+        rows = pl.ds(64 + 8 * v, 8)
+        marks_a[rows, :] = jnp.where(address < 65536, 2 * (address - index - 1024 * v) + 1, 0)
+        for c in range(3):
+            loads_a[c, rows, :] = tiles[v][1 + c]
     lane = lane_index(64)
     marks, values = (marks_a, marks_b), (loads_a, loads_b)
     for bit in range(15, -1, -1):
@@ -643,33 +701,29 @@
         load_now, load_later = values[bit % 2 == 0], values[bit % 2]
         test = 2 << bit
         rows = (1 << bit) // LANES
-
-        def step(block, _, now=now, later=later, load_now=load_now, load_later=load_later, test=test, rows=rows, bit=bit):
-            base = pl.multiple_of(block * 64, 64)
+        for base in range(0, 512, 64):
             here = pl.ds(base + 64, 64)
+            own = now[here, :]
+            own = jnp.where((own & test) != 0, 0, own)
+            if rows >= 64 and base < rows:
+                later[here, :] = own
+                for c in range(3):
+                    load_later[c, here, :] = load_now[c, here, :]
+                continue
 
             def source(ref):
                 if rows:
-                    if rows >= 64:
-                        start = pl.multiple_of(jnp.maximum(base + 64 - rows, 0), 8)
-                        return ref[pl.ds(start, 64), :]
                     return ref[pl.ds(base + 64 - rows, 64), :]
-                near = pltpu.roll(ref[here, :], 1 << bit, 1)
-                before = pltpu.roll(ref[pl.ds(base + 63, 64), :], 1 << bit, 1)
-                return jnp.where(lane < (1 << bit), before, near)
-
-            own = now[here, :]
-            own = jnp.where((own & test) != 0, 0, own)
+                mixed = jnp.where(
+                    lane >= LANES - (1 << bit), ref[pl.ds(base + 63, 64), :], ref[here, :]
+                )
+                return pltpu.roll(mixed, 1 << bit, 1)
+
             there = source(now)
             come = (there & test) != 0
-            if rows >= 64:
-                come = come & (base >= rows)
             later[here, :] = jnp.where(come, there, own)
             for c in range(3):
                 load_later[c, here, :] = jnp.where(come, source(load_now.at[c]), load_now[c, here, :])
-            return 0
-
-        lax.fori_loop(0, 8, step, 0)
     for j in range(16):
         rows = pl.ds(64 + 32 * j, 32)
         moved = marks_a[rows, :] != 0
@@ -683,7 +737,7 @@
 ):
     smem = pl.BlockSpec(memory_space=pltpu.SMEM)
     vmem = pl.BlockSpec(memory_space=pltpu.VMEM)
-    odd = (lax.axis_index("cell") % 2).astype(jnp.int32).reshape(1)
+    place = jnp.stack([lax.axis_index("cell"), lax.axis_index("level")]).astype(jnp.int32)
     outgoing = pl.pallas_call(
         pack_kernel,
         in_specs=[smem] + [vmem] * 5,
@@ -692,7 +746,7 @@
         compiler_params=params(),
         name="pack",
     )(
-        odd,
+        place,
         mover_pos.reshape(2, 32, LANES),
         mover_strength.reshape(32, LANES),
         mover_owner.reshape(32, LANES),
@@ -712,7 +766,7 @@
         compiler_params=params(),
         name="settle",
     )(arrived, resident_pos, resident_strength)
-    return fields(own)
+    return fields(own, place)
 
 
 def solution(mesh):

time: 140 us -> 113 us (0.81)
  Pallas kernels: 90.4 us -> 69.5 us
  starting transfers between devices: 21.8 us -> 10.7 us
  waiting for transfers between devices: 4.31 us -> 9.92 us
    pallas_call x1, Pallas kernels: 15.7 us -> 7.2 us  [local(): pl.pallas_call(settle_kernel, out_shape=shape(3, 16, 32, LANES), scratch_...]
    pallas_call x2, Pallas kernels: 48.4 us -> 40.7 us  [the longest x1 37.6 us: fields(): pl.pallas_call(near_kernel, in_specs=[smem] + [vmem] * 6, out_shape=shape...]
    ppermute x4, starting transfers between devices: 11.7 us -> 5.18 us  [neighbours(): lax.ppermute(value, axis, [(i, (i + step) % size) for i in range(size)])]
    ppermute x4, waiting for transfers between devices: 1.81 us -> 7.42 us  [neighbours(): lax.ppermute(value, axis, [(i, (i + step) % size) for i in range(size)])]
    all_to_all x1, starting transfers between devices: 10.1 us -> 5.52 us  [fields(): gathered = lax.all_to_all(coarse, ('cell', 'level'), 0, 0, tiled=True)]
    pallas_call x1, Pallas kernels: 11.7 us -> 9.13 us  [fields(): pl.pallas_call(far_kernel, grid_spec=pltpu.PrefetchScalarGridSpec(num_sca...]
    pallas_call x1, Pallas kernels: 7.89 us -> 6.13 us  [fields(): pl.pallas_call(upward_kernel, out_shape=(shape(ROWS * FAMILY, LANES), sha...]
  transfers between devices with their start and end apart: 6 -> 6, of which waited for: 3 -> 4; matrix products, arithmetic and copies ran while one was open for 0% -> 0% of each run, Pallas kernels for 33% -> 34%
where the time goes in v3:
time: 113 us; the launch traced here: 112 us
  Pallas kernels  69.5 us (62%)
  blocking collectives  16.8 us (15%)
  starting transfers between devices  10.7 us (9%)
  waiting for transfers between devices  9.92 us (9%)
  local copies, waits for them, and re-layouts  4.62 us (4%)
    pallas_call x1, Pallas kernels, fields(): pl.pallas_call(near_kernel, in_specs=[smem] + [vmem] * 6, out_shape=shape...  37.6 us
    all_to_all x1, blocking collectives, local(): arrived = lax.all_to_all(outgoing, 'cell', 0, 0, tiled=True)  16.8 us
    pallas_call x1, Pallas kernels, fields(): pl.pallas_call(far_kernel, grid_spec=pltpu.PrefetchScalarGridSpec(num_sca...  9.13 us
    ppermute x4, waiting for transfers between devices, neighbours(): lax.ppermute(value, axis, [(i, (i + step) % size) for i in range(size)])  7.42 us
    pallas_call x1, Pallas kernels, local(): pl.pallas_call(settle_kernel, out_shape=shape(3, 16, 32, LANES), scratch_...  7.2 us
    pallas_call x1, Pallas kernels, local(): pl.pallas_call(pack_kernel, in_specs=[smem] + [vmem] * 5, out_shape=shape...  6.29 us
    pallas_call x1, Pallas kernels, fields(): pl.pallas_call(upward_kernel, out_shape=(shape(ROWS * FAMILY, LANES), sha...  6.13 us
    all_to_all x1, starting transfers between devices, fields(): gathered = lax.all_to_all(coarse, ('cell', 'level'), 0, 0, tiled=True)  5.52 us
  transfers between devices with their start and end apart: 6, of which 4 were waited for; matrix products, arithmetic and copies ran while one was open for 0% of the time, Pallas kernels for 34%

profile of v3, /device:TPU:0, one launch (start us, length us, event | category | flops | bytes accessed | tf_op | source)
XLA Modules:
  0.0 112.2 jit_solution(8213660633643746022)
XLA Ops:
  0.0 0.6 pad_add_fusion.place_ref.place
  0.6 6.3 %pack.1 = f32[16,4,8,128]{3,2,1,0:T(8,128)} custom-call(s32[2]{0:T(128)} %pad_add_fusion.place_ref.place, f32[2,32,128]{2,1,0:T(8,128)} %bitcast.20, f32[32,128]{1,0:T(8,128)} %bitcast.21, s32[32,128]{1,0:T(8,128)} %bitcast.22, s32[32,128]{1,0:T(8,128)} %bitcast.23, s32[32,128]{1,0:T(8,128)} %bitcast.24), custom_call_target="tpu_custom_call" | custom-call | tf_op jit(solution)/shard_map/pack/pallas_call | solution.py:741
  6.9 16.8 %all_to_all.16.arrived = f32[16,4,8,128]{3,2,1,0:T(8,128)} all-to-all(f32[16,4,8,128]{3,2,1,0:T(8,128)} %pack.1), channel_id=1, replica_groups=mesh['cell'=16,'level'=4,'rep'=2] {'cell'}, dimensions={0} | all-to-all | bytes 524288 | tf_op jit(solution)/shard_map/all_to_all | solution.py:756
  23.7 7.2 %settle.1.own = f32[3,16,32,128]{3,2,1,0:T(8,128)} custom-call(f32[16,4,8,128]{3,2,1,0:T(8,128)} %all_to_all.16.arrived, f32[2,16,32,128]{3,2,1,0:T(8,128)} %pos.1, f32[16,32,128]{2,1,0:T(8,128)} %strength.1), custom_call_target="tpu_custom_call" | custom-call | tf_op jit(solution)/shard_map/settle/pallas_call | solution.py:757
  30.9 0.0 collective-permute-start
  30.9 2.5 %collective-permute-done.other = f32[3,16,32,128]{3,2,1,0:T(8,128)S(1)} collective-permute-done((f32[3,16,32,128]{3,2,1,0:T(8,128)}, f32[3,16,32,128]{3,2,1,0:T(8,128)S(1)}, u32[]{:S(2)}, u32[]{:S(2)}) %collective-permute-start) | collective-permute-done | bytes 786464 | tf_op jit(solution)/shard_map/ppermute | solution.py:515
  33.4 0.0 copy-start
  33.4 0.9 copy-done
  34.3 6.1 %upward.1 = (f32[2480,128]{1,0:T(8,128)}, f32[2,112,128]{2,1,0:T(8,128)}, f32[64,128]{1,0:T(8,128)}) custom-call(f32[3,16,32,128]{3,2,1,0:T(8,128)} %settle.1.own, f32[3,16,32,128]{3,2,1,0:T(8,128)} %copy-done, bf16[256,128]{1,0:T(8,128)(2,1)} %constant.33.clone.split_ref, bf16[32,240]{1,0:T(8,128)(2,1)} %constant.34.clone.lift_ref, ...), custom_call_target="tpu_custom_call" | custom-call | tf_op jit(solution)/shard_map/upward/pallas_call | solution.py:519
  40.4 0.9 slice_bitcast_fusion.2
  41.3 1.3 %collective-permute-start.2 = (f32[112,128]{1,0:T(8,128)S(1)}, f32[112,128]{1,0:T(8,128)S(1)}, u32[]{:S(2)}, u32[]{:S(2)}) collective-permute-start(f32[112,128]{1,0:T(8,128)S(1)} %get-tuple-element.19), channel_id=1, source_target_pairs={{0,120},{8,0},{16,8},{24,16},{32,24},{40,32},{48,40},{56,48},{64,5... | collective-permute-start | bytes 172040 | tf_op jit(solution)/shard_map/ppermute | solution.py:509
  42.6 0.7 collective-permute-start.1
  43.4 2.2 %collective-permute-done.2.came_right = f32[112,128]{1,0:T(8,128)S(1)} collective-permute-done((f32[112,128]{1,0:T(8,128)S(1)}, f32[112,128]{1,0:T(8,128)S(1)}, u32[]{:S(2)}, u32[]{:S(2)}) %collective-permute-start.2) | collective-permute-done | bytes 57376 | tf_op jit(solution)/shard_map/ppermute | solution.py:509
  45.5 0.0 copy-start.4
  45.5 4.6 %collective-permute-done.1.came_left = f32[112,128]{1,0:T(8,128)S(1)} collective-permute-done((f32[112,128]{1,0:T(8,128)S(1)}, f32[112,128]{1,0:T(8,128)S(1)}, u32[]{:S(2)}, u32[]{:S(2)}) %collective-permute-start.1) | collective-permute-done | bytes 57376 | tf_op jit(solution)/shard_map/ppermute | solution.py:509
  50.1 0.0 copy-done.4
  50.1 0.6 copy-done.5
  50.7 3.1 %rows.1 = (f32[2,264,128]{2,1,0:T(8,128)}, f32[112,128]{1,0:T(8,128)}, f32[112,128]{1,0:T(8,128)}) custom-call(s32[2]{0:T(128)} %pad_add_fusion.place_ref.place, f32[3,16,32,128]{3,2,1,0:T(8,128)} %settle.1.own, f32[3,16,32,128]{3,2,1,0:T(8,128)} %copy-done, f32[2480,128]{1,0:T(8,128)} %get-tuple-element.11.cells, f32[112,128]{1,0:T(8,128)} %copy-done.5, ...), custom_call_target="tpu_custom_call" | custom-call | tf_op jit(solution)/shard_map/rows/pallas_call | solution.py:530
  53.9 1.0 slice_bitcast_fusion
  54.9 3.1 %collective-permute-start.4 = (f32[264,128]{1,0:T(8,128)S(1)}, f32[264,128]{1,0:T(8,128)S(1)}, u32[]{:S(2)}, u32[]{:S(2)}) collective-permute-start(f32[264,128]{1,0:T(8,128)S(1)} %get-tuple-element.17), channel_id=1, source_target_pairs={{0,6},{2,0},{4,2},{6,4},{1,7},{3,1},{5,3},{7,5},{8,14},{10,8},{12,... | collective-permute-start | bytes 405512 | tf_op jit(solution)/shard_map/ppermute | solution.py:509
  57.9 0.0 collective-permute-start.3
  57.9 5.5 %all-to-all-start.1 = ((f32[64,1,128]{2,1,0:T(1,128)}), f32[64,1,128]{2,1,0:T(1,128)S(1)}, u32[]{:S(2)}, u32[]{:S(2)}) async-start(f32[64,1,128]{2,1,0:T(1,128)} %bitcast.12), calls=%async_computation.1 | async-start | bytes 65536 | tf_op jit(solution)/shard_map/all_to_all | solution.py:528
  63.5 0.0 collective-permute-done.4.came_below.below
  63.5 0.0 copy-start.1
  63.5 0.7 collective-permute-done.3.came_above.above
  64.2 0.0 copy-start.2
  64.2 0.0 copy-done.1
  64.2 0.6 copy-done.2
  64.8 37.6 %near.1 = f32[2,16,32,128]{3,2,1,0:T(8,128)} custom-call(s32[2]{0:T(128)} %pad_add_fusion.place_ref.place, f32[3,16,32,128]{3,2,1,0:T(8,128)} %settle.1.own, f32[3,16,32,128]{3,2,1,0:T(8,128)} %copy-done, f32[112,128]{1,0:T(8,128)} %get-tuple-element.13.from_left, f32[112,128]{1,0:T(8,128)} %get-tuple-element.14.from_right, f32[264,128]{1,0:T(8,128)} %copy-done.2, ...), custom_call_target="tpu_custom_call" | custom-call | tf_op jit(solution)/shard_map/near/pallas_call | solution.py:539
  102.4 0.0 all-to-all-done.1
  102.4 0.6 copy-done.3
  103.0 9.1 %far.1 = f32[2,16,32,128]{3,2,1,0:T(8,128)} custom-call(s32[2]{0:T(128)} %pad_add_fusion.place_ref.place, f32[3,16,32,128]{3,2,1,0:T(8,128)} %settle.1.own, f32[2,16,32,128]{3,2,1,0:T(8,128)} %near.1, f32[2480,128]{1,0:T(8,128)} %get-tuple-element.11.cells, f32[112,128]{1,0:T(8,128)} %get-tuple-element.13.from_left, ...), custom_call_target="tpu_custom_call" | custom-call | tf_op jit(solution)/shard_map/far/pallas_call | solution.py:572
  (2 shorter events, 0.0 us)
Async XLA Ops:
  30.9 2.5 %collective-permute-start = (f32[3,16,32,128]{3,2,1,0:T(8,128)}, f32[3,16,32,128]{3,2,1,0:T(8,128)S(1)}, u32[]{:S(2)}, u32[]{:S(2)}) collective-permute-start(f32[3,16,32,128]{3,2,1,0:T(8,128)} %settle.1.own), channel_id=1, source_target_pairs={{0,1},{1,0},{2,3},{3,2},{4,5},{5,4},{6,7},{7,6},{8,9},{9,8},{10,11... | collective-permute-start | bytes 2359304 | tf_op jit(solution)/shard_map/ppermute | solution.py:515
  33.4 0.9 copy-start
  41.3 4.2 %collective-permute-start.2 = (f32[112,128]{1,0:T(8,128)S(1)}, f32[112,128]{1,0:T(8,128)S(1)}, u32[]{:S(2)}, u32[]{:S(2)}) collective-permute-start(f32[112,128]{1,0:T(8,128)S(1)} %get-tuple-element.19), channel_id=1, source_target_pairs={{0,120},{8,0},{16,8},{24,16},{32,24},{40,32},{48,40},{56,48},{64,5... | collective-permute-start | bytes 172040 | tf_op jit(solution)/shard_map/ppermute | solution.py:509
  42.6 7.5 %collective-permute-start.1 = (f32[112,128]{1,0:T(8,128)S(1)}, f32[112,128]{1,0:T(8,128)S(1)}, u32[]{:S(2)}, u32[]{:S(2)}) collective-permute-start(f32[112,128]{1,0:T(8,128)S(1)} %get-tuple-element.20), channel_id=1, source_target_pairs={{0,8},{8,16},{16,24},{24,32},{32,40},{40,48},{48,56},{56,64},{64,7... | collective-permute-start | bytes 172040 | tf_op jit(solution)/shard_map/ppermute | solution.py:509
  45.5 4.6 %copy-start.4 = (f32[112,128]{1,0:T(8,128)}, f32[112,128]{1,0:T(8,128)S(1)}, u32[]{:S(2)}) copy-start(f32[112,128]{1,0:T(8,128)S(1)} %collective-permute-done.2.came_right) | copy-start | bytes 172036
  50.1 0.6 copy-start.5
  54.9 8.6 %collective-permute-start.4 = (f32[264,128]{1,0:T(8,128)S(1)}, f32[264,128]{1,0:T(8,128)S(1)}, u32[]{:S(2)}, u32[]{:S(2)}) collective-permute-start(f32[264,128]{1,0:T(8,128)S(1)} %get-tuple-element.17), channel_id=1, source_target_pairs={{0,6},{2,0},{4,2},{6,4},{1,7},{3,1},{5,3},{7,5},{8,14},{10,8},{12,... | collective-permute-start | bytes 405512 | tf_op jit(solution)/shard_map/ppermute | solution.py:509
  57.9 6.2 %collective-permute-start.3 = (f32[264,128]{1,0:T(8,128)S(1)}, f32[264,128]{1,0:T(8,128)S(1)}, u32[]{:S(2)}, u32[]{:S(2)}) collective-permute-start(f32[264,128]{1,0:T(8,128)S(1)} %get-tuple-element.18), channel_id=1, source_target_pairs={{0,2},{2,4},{4,6},{6,0},{1,3},{3,5},{5,7},{7,1},{8,10},{10,12},{12... | collective-permute-start | bytes 405512 | tf_op jit(solution)/shard_map/ppermute | solution.py:509
  57.9 44.5 %all-to-all-start.1 = ((f32[64,1,128]{2,1,0:T(1,128)}), f32[64,1,128]{2,1,0:T(1,128)S(1)}, u32[]{:S(2)}, u32[]{:S(2)}) async-start(f32[64,1,128]{2,1,0:T(1,128)} %bitcast.12), calls=%async_computation.1 | async-start | bytes 65536 | tf_op jit(solution)/shard_map/all_to_all | solution.py:528
  63.5 0.7 copy-start.1
  64.2 0.6 copy-start.2
  102.4 0.6 copy-start.3

commit v4 on v3

--- a/solution.py
+++ b/solution.py
@@ -184,7 +184,7 @@
 
 
 def upward_kernel(
-    own, other, split_ref, lift_ref, spread_ref, cells, packed, coarse, mom, raw
+    after, own, other, split_ref, lift_ref, spread_ref, cells, to_left, to_right, top, bottom, coarse, mom, raw
 ):
     for tile in range(4):
         rows = pl.ds(8 * tile, 8)
@@ -215,6 +215,7 @@
     lane80 = lane_index(FAMILY)
     first = jnp.zeros((FAMILY, LANES), f32)
     last = jnp.zeros((FAMILY, LANES), f32)
+    ends = [jnp.zeros((FAMILY, LANES), f32)] * 2
     for k, height in enumerate(HEIGHTS):
         source = mom[...] if k == 0 else raw[pl.ds(0, 40 * height), :]
         spread = dot(jnp.concatenate(halves(source), axis=1), split_ref[...])
@@ -231,12 +232,27 @@
                 lane80 == index, pltpu.roll(parent, (index - WIDTHS[k] + 1) % LANES, 1), last
             )
             parents.append(parent)
+            for side, ref in enumerate((top, bottom)):
+                if row != (height - 1) * side:
+                    continue
+                if k == 0:
+                    ref[pl.ds(104, FAMILY), :] = parent
+                else:
+                    inside = (lane80 > PACKS[k]) & (lane80 <= PACKS[k] + WIDTHS[k])
+                    ends[side] = jnp.where(inside, pltpu.roll(parent, PACKS[k] + 1, 1), ends[side])
         high, low = halves(jnp.concatenate(parents, axis=1))
         lifted = dot(lift_ref[...], jnp.concatenate([high, low, high], axis=0))
         for row in range(height):
             raw[pl.ds(CHAN * row, CHAN), :] = lifted[:CHAN, LANES * row : LANES * (row + 1)]
-    packed[0, pl.ds(32, FAMILY), :] = first
-    packed[1, pl.ds(32, FAMILY), :] = last
+    to_left[pl.ds(32, FAMILY), :] = first
+    to_right[pl.ds(32, FAMILY), :] = last
+    for side, ref in enumerate((top, bottom)):
+        ref[pl.ds(104 + FAMILY, FAMILY), :] = ends[side]
+        ref[pl.ds(96, 8), :] = jnp.zeros((8, LANES), f32)
+        for half, source in enumerate((own, other)):
+            for comp in range(3):
+                for j in range(16):
+                    ref[pl.ds(comp * 32 + half * 16 + j, 1), :] = source[comp, j, pl.ds(31 * side, 1), :]
 
     four = jnp.dot(raw[pl.ds(0, 24), :], spread_ref[...], precision=precise)
     row24 = lax.broadcasted_iota(jnp.int32, (24, LANES), 0)
@@ -253,8 +269,8 @@
                 value = ref[comp, j]
                 left = jnp.where(lane32 == m, pltpu.roll(value, m, 1), left)
                 right = jnp.where(lane32 == m, pltpu.roll(value, m + 1, 1), right)
-    packed[0, pl.ds(0, 32), :] = left
-    packed[1, pl.ds(0, 32), :] = right
+    to_left[pl.ds(0, 32), :] = left
+    to_right[pl.ds(0, 32), :] = right
 
 
 def ring_columns(parent, k, index, from_left, from_right, lane):
@@ -263,38 +279,89 @@
     return jnp.where(lane == width, pltpu.roll(from_right, (width - index) % LANES, 1), parent)
 
 
-def rows_kernel(place, own, other, cells, came_left, came_right, out, from_left, from_right):
+def rows_kernel(place, after, top, bottom, came_left, came_right, out_top, out_bottom, from_left, from_right):
     lane80 = lane_index(FAMILY)
     from_left[...] = jnp.where(place[0] > 0, came_left[...], 0.0)
     from_right[...] = jnp.where(place[0] < 15, came_right[...], 0.0)
     left, right = from_left[pl.ds(32, FAMILY), :], from_right[pl.ds(32, FAMILY), :]
-    for side in (0, 1):
-        row = 31 * side
-        for comp in range(3):
-            for half, ref in enumerate((own, other)):
-                for j in range(16):
-                    out[side, pl.ds(comp * 32 + half * 16 + j, 1), :] = ref[comp, j, pl.ds(row, 1), :]
-        out[side, pl.ds(96, 1), :] = from_left[pl.ds(row, 1), :]
-        out[side, pl.ds(97, 1), :] = from_right[pl.ds(row, 1), :]
-        out[side, pl.ds(98, 6), :] = jnp.zeros((6, LANES), f32)
-        packed = jnp.zeros((FAMILY, LANES), f32)
-        for k, height in enumerate(HEIGHTS):
-            index = OFFSETS[k] + (height - 1) * side
-            parent = cells[pl.ds(FAMILY * index, FAMILY), :]
-            parent = ring_columns(parent, k, index, left, right, lane80)
-            if k == 0:
-                out[side, pl.ds(104, FAMILY), :] = parent
+    for side, (ref, out) in enumerate(((top, out_top), (bottom, out_bottom))):
+        out[pl.ds(0, 104), :] = ref[pl.ds(0, 104), :]
+        out[pl.ds(96, 1), :] = from_left[pl.ds(31 * side, 1), :]
+        out[pl.ds(97, 1), :] = from_right[pl.ds(31 * side, 1), :]
+        out[pl.ds(104, FAMILY), :] = ring_columns(
+            ref[pl.ds(104, FAMILY), :], 0, 15 * side, left, right, lane80
+        )
+        packed = ref[pl.ds(104 + FAMILY, FAMILY), :]
+        for k in range(1, 5):
+            index = OFFSETS[k] + (HEIGHTS[k] - 1) * side
+            start = PACKS[k]
+            stop = start + WIDTHS[k] + 1
+            packed = jnp.where(lane80 == start, pltpu.roll(left, (start - index) % LANES, 1), packed)
+            packed = jnp.where(lane80 == stop, pltpu.roll(right, (stop - index) % LANES, 1), packed)
+        out[pl.ds(104 + FAMILY, FAMILY), :] = packed
+
+
+GROUP = 8
+
+
+def inside_domain(tile, dy):
+    return dy == 0 or (dy == -1 and tile > 0) or (dy == 1 and tile < 3)
+
+
+def add_sources(acc, own, tile, group, sources, count, unroll):
+    rows = pl.ds(8 * tile, 8)
+    tx = [own[0, group * GROUP + i, rows, :] for i in range(GROUP)]
+    ty = [own[1, group * GROUP + i, rows, :] for i in range(GROUP)]
+
+    def pairs(j, acc):
+        acc = list(acc)
+        for source in sources:
+            sx, sy, q = source(j)
+            for i in range(GROUP):
+                gap_x = tx[i] - sx
+                gap_y = ty[i] - sy
+                weight = q * (1.0 / (gap_x * gap_x + (gap_y * gap_y + BLOB)))
+                acc[i] = acc[i] + weight * gap_x
+                acc[GROUP + i] = acc[GROUP + i] + weight * gap_y
+        return tuple(acc)
+
+    return lax.fori_loop(0, count, pairs, acc, unroll=unroll)
+
+
+def store_group(out, acc, tile, group):
+    for i in range(GROUP):
+        out[0, group * GROUP + i, pl.ds(8 * tile, 8), :] = acc[i]
+        out[1, group * GROUP + i, pl.ds(8 * tile, 8), :] = acc[GROUP + i]
+
+
+def inner_kernel(own, sources, earlier, after, out, *, add):
+    for tile in range(4):
+        for group in range(16 // GROUP):
+            if add:
+                acc = tuple(
+                    earlier[part, group * GROUP + i, pl.ds(8 * tile, 8), :]
+                    for part in range(2)
+                    for i in range(GROUP)
+                )
             else:
-                moved = pltpu.roll(parent, PACKS[k] + 1, 1)
-                inside = (lane80 >= PACKS[k]) & (lane80 < PACKS[k] + WIDTHS[k] + 2)
-                packed = jnp.where(inside, moved, packed)
-        out[side, pl.ds(104 + FAMILY, FAMILY), :] = packed
-
-
-GROUP = 8
-
-
-def near_kernel(place, own, other, from_left, from_right, came_above, came_below, out, src, above, below):
+                acc = tuple(jnp.zeros((8, LANES), f32) for _ in range(2 * GROUP))
+            steps = []
+            for dy in (-1, 0, 1):
+                if not inside_domain(tile, dy):
+                    continue
+
+                def source(j, rows=pl.ds(8 * tile + dy, 8), dy=dy):
+                    y = sources[1, j, rows, :]
+                    return sources[0, j, rows, :], y + float(dy) if dy else y, sources[2, j, rows, :]
+
+                steps.append(source)
+            acc = add_sources(acc, own, tile, group, steps, 16, 4)
+            store_group(out, acc, tile, group)
+
+
+def near_kernel(
+    place, own, other, inner, from_left, from_right, came_above, came_below, out, src, above, below
+):
     above[...] = jnp.where(place[1] > 0, came_above[pl.ds(0, 104), :], 0.0)
     below[...] = jnp.where(place[1] < 3, came_below[pl.ds(0, 104), :], 0.0)
     lane32 = lane_index(32)
@@ -326,29 +393,24 @@
 
     for tile in range(4):
         for group in range(16 // GROUP):
-            tx = [own[0, group * GROUP + i, pl.ds(8 * tile, 8), :] for i in range(GROUP)]
-            ty0 = [own[1, group * GROUP + i, pl.ds(8 * tile, 8), :] for i in range(GROUP)]
-            acc = tuple(jnp.zeros((8, LANES), f32) for _ in range(2 * GROUP))
+            acc = tuple(
+                inner[part, group * GROUP + i, pl.ds(8 * tile, 8), :]
+                for part in range(2)
+                for i in range(GROUP)
+            )
+            steps = []
             for dy in (-1, 0, 1):
-                ty = [value - float(dy) for value in ty0] if dy else ty0
-                rows = pl.ds(8 + 8 * tile + dy, 8)
                 for dx in range(3):
-
-                    def pairs(j, acc, dx=dx, rows=rows, ty=ty, tx=tx):
-                        acc = list(acc)
-                        sx, sy, q = src[dx, j, rows, :], src[dx, 32 + j, rows, :], src[dx, 64 + j, rows, :]
-                        for i in range(GROUP):
-                            gap_x = tx[i] - sx
-                            gap_y = ty[i] - sy
-                            weight = q * (1.0 / (gap_x * gap_x + (gap_y * gap_y + BLOB)))
-                            acc[i] = acc[i] + weight * gap_x
-                            acc[GROUP + i] = acc[GROUP + i] + weight * gap_y
-                        return tuple(acc)
-
-                    acc = lax.fori_loop(0, 32, pairs, acc, unroll=8)
-            for i in range(GROUP):
-                out[0, group * GROUP + i, pl.ds(8 * tile, 8), :] = acc[i]
-                out[1, group * GROUP + i, pl.ds(8 * tile, 8), :] = acc[GROUP + i]
+                    if dx == 1 and inside_domain(tile, dy):
+                        continue
+
+                    def source(j, dx=dx, rows=pl.ds(8 + 8 * tile + dy, 8), dy=dy):
+                        y = src[dx, 32 + j, rows, :]
+                        return src[dx, j, rows, :], y + float(dy) if dy else y, src[dx, 64 + j, rows, :]
+
+                    steps.append(source)
+            acc = add_sources(acc, own, tile, group, steps, 32, 2)
+            store_group(out, acc, tile, group)
 
 
 def three_products(value, table):
@@ -512,33 +574,49 @@
 def fields(own, place):
     smem = pl.BlockSpec(memory_space=pltpu.SMEM)
     vmem = pl.BlockSpec(memory_space=pltpu.VMEM)
+    anywhere = pl.BlockSpec(memory_space=pl.ANY)
     other = lax.ppermute(own, "rep", [(0, 1), (1, 0)])
+    inner = pl.pallas_call(
+        lambda own, out: inner_kernel(own, own, None, None, out, add=False),
+        out_shape=shape(2, 16, 32, LANES),
+        compiler_params=params(),
+        name="inner_own",
+    )(own)
     lift_high, lift_low = halves_np(upward_family())
     lift = np.zeros((32, 3 * FAMILY), jnp.bfloat16)
     lift[:CHAN] = np.concatenate([lift_high, lift_high, lift_low], axis=1)
-    cells, packed, coarse = pl.pallas_call(
+    message = shape(104 + 2 * FAMILY, LANES)
+    sides = shape(32 + FAMILY, LANES)
+    cells, to_left, to_right, top, bottom, coarse = pl.pallas_call(
         upward_kernel,
-        out_shape=(shape(ROWS * FAMILY, LANES), shape(2, 32 + FAMILY, LANES), shape(64, LANES)),
+        in_specs=[anywhere] + [vmem] * 5,
+        out_shape=(shape(ROWS * FAMILY, LANES), sides, sides, message, message, shape(64, LANES)),
         scratch_shapes=[pltpu.VMEM((640, LANES), f32), pltpu.VMEM((320, LANES), f32)],
         compiler_params=params(),
         name="upward",
-    )(own, other, jnp.asarray(split_lanes()), jnp.asarray(lift), jnp.asarray(quarter_lanes().T.copy()))
-    from_left = neighbours(packed[1], "cell", 1)
-    from_right = neighbours(packed[0], "cell", -1)
+    )(inner, own, other, jnp.asarray(split_lanes()), jnp.asarray(lift), jnp.asarray(quarter_lanes().T.copy()))
+    from_left = neighbours(to_right, "cell", 1)
+    from_right = neighbours(to_left, "cell", -1)
     gathered = lax.all_to_all(coarse, ("cell", "level"), 0, 0, tiled=True)
-    sides = shape(32 + FAMILY, LANES)
-    rows, from_left, from_right = pl.pallas_call(
+    inner = pl.pallas_call(
+        functools.partial(inner_kernel, add=True),
+        in_specs=[vmem] * 3 + [anywhere],
+        out_shape=shape(2, 16, 32, LANES),
+        compiler_params=params(),
+        name="inner",
+    )(own, other, inner, cells)
+    top, bottom, from_left, from_right = pl.pallas_call(
         rows_kernel,
-        in_specs=[smem] + [vmem] * 5,
-        out_shape=(shape(2, 104 + 2 * FAMILY, LANES), sides, sides),
+        in_specs=[smem, anywhere] + [vmem] * 4,
+        out_shape=(message, message, sides, sides),
         compiler_params=params(),
         name="rows",
-    )(place, own, other, cells, from_left, from_right)
-    above = neighbours(rows[1], "level", 1)
-    below = neighbours(rows[0], "level", -1)
+    )(place, inner, top, bottom, from_left, from_right)
+    above = neighbours(bottom, "level", 1)
+    below = neighbours(top, "level", -1)
     near = pl.pallas_call(
         near_kernel,
-        in_specs=[smem] + [vmem] * 6,
+        in_specs=[smem] + [vmem] * 7,
         out_shape=shape(2, 16, 32, LANES),
         scratch_shapes=[
             pltpu.VMEM((3, 96, 48, LANES), f32),
@@ -547,7 +625,7 @@
         ],
         compiler_params=params(),
         name="near",
-    )(place, own, other, from_left, from_right, above, below)
+    )(place, own, other, inner, from_left, from_right, above, below)
     far_high, far_low = halves_np(far_family())
     drop_table = np.zeros((FAMILY, 32))
     drop_table[:, :CHAN] = downward_family()
@@ -643,25 +721,22 @@
     return tiles
 
 
-def pack_kernel(place_ref, pos, strength, owner_ref, leaf, slot, out, keys, values):
-    odd = place_ref[0] % 2
+def pack_kernel(pos, strength, owner_ref, leaf, slot, out, keys, values):
     owner = owner_ref[...]
     address = slot[...] * 4096 + leaf[...]
-    address = jnp.where(odd == 1, 65535 - address, address)
     key = owner * 65536 + address
     starts = []
     for o in range(16):
-        bound = jnp.where(odd == 1, o + 1, o)
-        before = (owner < bound).astype(jnp.int32)
+        before = (owner < o).astype(jnp.int32)
         before = before[0:8] + before[8:16] + before[16:24] + before[24:32]
-        starts.append(jnp.sum(before) + jnp.where(odd == 1, 0, 1024))
+        starts.append(jnp.sum(before))
     loads = (key, pos[0], pos[1], strength[...])
     tiles = bitonic([[load[8 * v : 8 * v + 8] for load in loads] for v in range(4)], 1, 12)
     keys[...] = jnp.full(keys.shape, -1, jnp.int32)
     for v in range(4):
-        keys[pl.ds(8 + 8 * v, 8), :] = tiles[v][0]
+        keys[pl.ds(8 * v, 8), :] = tiles[v][0]
         for c in range(3):
-            values[c, pl.ds(8 + 8 * v, 8), :] = tiles[v][1 + c]
+            values[c, pl.ds(8 * v, 8), :] = tiles[v][1 + c]
     lane = lane_index(8)
     for o in range(16):
         start = starts[o]
@@ -670,21 +745,25 @@
         back = jnp.where(shift == 0, 0, LANES - shift)
 
         def window(ref):
-            upper = pltpu.roll(ref[pl.ds(row, 8), :], back, 1)
-            lower = pltpu.roll(ref[pl.ds(row + 1, 8), :], back, 1)
-            return jnp.where(lane < LANES - shift, upper, lower)
+            mixed = jnp.where(lane < shift, ref[pl.ds(row + 1, 8), :], ref[pl.ds(row, 8), :])
+            return pltpu.roll(mixed, back, 1)
 
         mine = window(keys)
         place = mine - o * 65536
         valid = (place >= 0) & (place < 65536)
-        place = jnp.where(odd == 1, 65535 - place, place)
         out[o, 3] = jnp.where(valid, place, 65536).astype(f32)
         for c in range(3):
             out[o, c] = window(values.at[c])
 
 
 def settle_kernel(arrived, pos, strength, out, marks_a, marks_b, loads_a, loads_b):
-    tiles = bitonic([[arrived[v, c] for c in (3, 0, 1, 2)] for v in range(16)], 11, 14)
+    tiles = [[arrived[v, c] for c in (3, 0, 1, 2)] for v in range(16)]
+    turned = [lax.broadcasted_iota(jnp.int32, (8, LANES), axis) for axis in (0, 1)]
+    for v in range(1, 16, 2):
+        for c in range(4):
+            value = jnp.take_along_axis(tiles[v][c], 7 - turned[0], axis=0)
+            tiles[v][c] = jnp.take_along_axis(value, LANES - 1 - turned[1], axis=1)
+    tiles = bitonic(tiles, 11, 14)
     index = flat_index((8, LANES))
     for ref in (marks_a, marks_b):
         ref[...] = jnp.zeros(ref.shape, jnp.int32)
@@ -735,18 +814,14 @@
 def local(
     resident_pos, resident_strength, mover_pos, mover_strength, mover_owner, mover_leaf, mover_slot
 ):
-    smem = pl.BlockSpec(memory_space=pltpu.SMEM)
-    vmem = pl.BlockSpec(memory_space=pltpu.VMEM)
     place = jnp.stack([lax.axis_index("cell"), lax.axis_index("level")]).astype(jnp.int32)
     outgoing = pl.pallas_call(
         pack_kernel,
-        in_specs=[smem] + [vmem] * 5,
         out_shape=shape(16, 4, 8, LANES),
         scratch_shapes=[pltpu.VMEM((56, LANES), jnp.int32), pltpu.VMEM((3, 56, LANES), f32)],
         compiler_params=params(),
         name="pack",
     )(
-        place,
         mover_pos.reshape(2, 32, LANES),
         mover_strength.reshape(32, LANES),
         mover_owner.reshape(32, LANES),

time: 113 us -> 106 us (0.938)
  waiting for transfers between devices: 9.92 us -> 0.02 us
  starting transfers between devices: 10.7 us -> 13.2 us
  local copies, waits for them, and re-layouts: 4.62 us -> 2.8 us
  Pallas kernels: 69.5 us -> 71.2 us
    ppermute x4, waiting for transfers between devices: 7.42 us -> 0.01 us  [neighbours(): lax.ppermute(value, axis, [(i, (i + step) % size) for i in range(size)])]
    ppermute x4, starting transfers between devices: 5.18 us -> 8.58 us  [neighbours(): lax.ppermute(value, axis, [(i, (i + step) % size) for i in range(size)])]
    ppermute x1, waiting for transfers between devices: 2.49 us -> 0.01 us  [fields(): other = lax.ppermute(own, 'rep', [(0, 1), (1, 0)])]
    squeeze x2 -> x0, local copies, waits for them, and re-layouts: 1.84 us -> none  [the longest x1 0.99 us: fields(): below = neighbours(rows[0], 'level', -1)]
    pallas_call x4 -> x6, Pallas kernels: 53.2 us -> 54.8 us  [the longest x1 27.2 us: fields(): pl.pallas_call(near_kernel, in_specs=[smem] + [vmem] * 7, out_shape=shape...]
  transfers between devices with their start and end apart: 6 -> 6, of which waited for: 4 -> 0; matrix products, arithmetic and copies ran while one was open for 0% -> 1% of each run, Pallas kernels for 34% -> 39%
where the time goes in v4:
time: 106 us; the launch traced here: 105 us
  Pallas kernels  71.2 us (67%)
  blocking collectives  16.8 us (16%)
  starting transfers between devices  13.2 us (12%)
  local copies, waits for them, and re-layouts  2.8 us (3%)
    pallas_call x1, Pallas kernels, fields(): pl.pallas_call(near_kernel, in_specs=[smem] + [vmem] * 7, out_shape=shape...  27.2 us
    all_to_all x1, blocking collectives, local(): arrived = lax.all_to_all(outgoing, 'cell', 0, 0, tiled=True)  16.8 us
    pallas_call x1, Pallas kernels, fields(): pl.pallas_call(far_kernel, grid_spec=pltpu.PrefetchScalarGridSpec(num_sca...  9.14 us
    ppermute x4, starting transfers between devices, neighbours(): lax.ppermute(value, axis, [(i, (i + step) % size) for i in range(size)])  8.58 us
    pallas_call x1, Pallas kernels, local(): pl.pallas_call(settle_kernel, out_shape=shape(3, 16, 32, LANES), scratch_...  7.29 us
    pallas_call x1, Pallas kernels, fields(): pl.pallas_call(functools.partial(inner_kernel, add=True), in_specs=[vmem]...  6.85 us
    pallas_call x1, Pallas kernels, fields(): pl.pallas_call(lambda own, out: inner_kernel(own, own, None, None, out, a...  6.4 us
    pallas_call x1, Pallas kernels, local(): pl.pallas_call(pack_kernel, out_shape=shape(16, 4, 8, LANES), scratch_sha...  6.27 us
  transfers between devices with their start and end apart: 6, of which 0 were waited for; matrix products, arithmetic and copies ran while one was open for 1% of the time, Pallas kernels for 39%

profile of v4, /device:TPU:0, one launch (start us, length us, event | category | flops | bytes accessed | tf_op | source)
XLA Modules:
  0.0 104.7 jit_solution(9199320433531118166)
XLA Ops:
  0.0 6.3 %pack.1 = f32[16,4,8,128]{3,2,1,0:T(8,128)} custom-call(f32[2,32,128]{2,1,0:T(8,128)} %bitcast.12, f32[32,128]{1,0:T(8,128)} %bitcast.13, s32[32,128]{1,0:T(8,128)} %bitcast.14, s32[32,128]{1,0:T(8,128)} %bitcast.15, s32[32,128]{1,0:T(8,128)} %bitcast.16), custom_call_target="tpu_custom_call" | custom-call | tf_op jit(solution)/shard_map/pack/pallas_call | solution.py:818
  6.3 16.8 %all_to_all.16.arrived = f32[16,4,8,128]{3,2,1,0:T(8,128)} all-to-all(f32[16,4,8,128]{3,2,1,0:T(8,128)} %pack.1), channel_id=1, replica_groups=mesh['cell'=16,'level'=4,'rep'=2] {'cell'}, dimensions={0} | all-to-all | bytes 524288 | tf_op jit(solution)/shard_map/all_to_all | solution.py:831
  23.0 7.3 %settle.1.own = f32[3,16,32,128]{3,2,1,0:T(8,128)} custom-call(f32[16,4,8,128]{3,2,1,0:T(8,128)} %all_to_all.16.arrived, f32[2,16,32,128]{3,2,1,0:T(8,128)} %pos.1, f32[16,32,128]{2,1,0:T(8,128)} %strength.1), custom_call_target="tpu_custom_call" | custom-call | tf_op jit(solution)/shard_map/settle/pallas_call | solution.py:832
  30.3 0.0 collective-permute-start
  30.3 6.4 %inner_own.1.after.earlier = f32[2,16,32,128]{3,2,1,0:T(8,128)} custom-call(f32[3,16,32,128]{3,2,1,0:T(8,128)} %settle.1.own), custom_call_target="tpu_custom_call" | custom-call | tf_op jit(solution)/shard_map/inner_own/pallas_call | solution.py:579
  36.7 0.0 collective-permute-done.other.sources
  36.7 0.0 copy-start
  36.7 0.9 copy-done
  37.6 6.2 %upward.1 = (f32[2480,128]{1,0:T(8,128)}, f32[112,128]{1,0:T(8,128)}, f32[112,128]{1,0:T(8,128)}, f32[264,128]{1,0:T(8,128)}, f32[264,128]{1,0:T(8,128)}, /*index=5*/f32[64,128]{1,0:T(8,128)}) custom-call(f32[2,16,32,128]{3,2,1,0:T(8,128)} %inner_own.1.after.earlier, f32[3,16,32,128]{3,2,1,0:T(8,128)} %settle.1.own, f32[3,16,32,128]{3,2,1,0:T(8,128)} %copy-done, ...), custom_call_target="tpu_custom_call" | custom-call | tf_op jit(solution)/shard_map/upward/pallas_call | solution.py:590
  43.8 0.6 collective-permute-start.1
  44.4 4.8 %collective-permute-start.2 = (f32[112,128]{1,0:T(8,128)}, f32[112,128]{1,0:T(8,128)S(1)}, u32[]{:S(2)}, u32[]{:S(2)}) collective-permute-start(f32[112,128]{1,0:T(8,128)} %get-tuple-element.19), channel_id=1, source_target_pairs={{0,120},{8,0},{16,8},{24,16},{32,24},{40,32},{48,40},{56,48},{64,5... | collective-permute-start | bytes 172040 | tf_op jit(solution)/shard_map/ppermute | solution.py:571
  49.2 0.6 pad_add_fusion.place
  49.8 6.9 %inner.1.after = f32[2,16,32,128]{3,2,1,0:T(8,128)} custom-call(f32[3,16,32,128]{3,2,1,0:T(8,128)} %settle.1.own, f32[3,16,32,128]{3,2,1,0:T(8,128)} %copy-done, f32[2,16,32,128]{3,2,1,0:T(8,128)} %inner_own.1.after.earlier, f32[2480,128]{1,0:T(8,128)} %get-tuple-element.15.after.cells), custom_call_target="tpu_custom_call" | custom-call | tf_op jit(solution)/shard_map/inner/pallas_call | solution.py:601
  56.7 0.0 collective-permute-done.1.came_left
  56.7 0.0 collective-permute-done.2.came_right
  56.7 0.0 copy-start.5
  56.7 0.6 copy-done.4
  57.3 0.0 copy-done.5
  57.4 1.9 %rows.1 = (f32[264,128]{1,0:T(8,128)}, f32[264,128]{1,0:T(8,128)}, f32[112,128]{1,0:T(8,128)}, f32[112,128]{1,0:T(8,128)}) custom-call(s32[2]{0:T(128)} %pad_add_fusion.place, f32[2,16,32,128]{3,2,1,0:T(8,128)} %inner.1.after, f32[264,128]{1,0:T(8,128)} %get-tuple-element.16.top, f32[264,128]{1,0:T(8,128)} %get-tuple-element.17.bottom, ...), custom_call_target="tpu_custom_call" | custom-call | tf_op jit(solution)/shard_map/rows/pallas_call | solution.py:608
  59.3 1.6 %collective-permute-start.3 = (f32[264,128]{1,0:T(8,128)}, f32[264,128]{1,0:T(8,128)S(1)}, u32[]{:S(2)}, u32[]{:S(2)}) collective-permute-start(f32[264,128]{1,0:T(8,128)} %get-tuple-element.22), channel_id=1, source_target_pairs={{0,2},{2,4},{4,6},{6,0},{1,3},{3,5},{5,7},{7,1},{8,10},{10,12},{12... | collective-permute-start | bytes 405512 | tf_op jit(solution)/shard_map/ppermute | solution.py:571
  60.8 1.7 %collective-permute-start.4 = (f32[264,128]{1,0:T(8,128)}, f32[264,128]{1,0:T(8,128)S(1)}, u32[]{:S(2)}, u32[]{:S(2)}) collective-permute-start(f32[264,128]{1,0:T(8,128)} %get-tuple-element.23), channel_id=1, source_target_pairs={{0,6},{2,0},{4,2},{6,4},{1,7},{3,1},{5,3},{7,5},{8,14},{10,8},{12,... | collective-permute-start | bytes 405512 | tf_op jit(solution)/shard_map/ppermute | solution.py:571
  62.5 4.6 %all-to-all-start.1 = ((f32[64,1,128]{2,1,0:T(1,128)}), f32[64,1,128]{2,1,0:T(1,128)S(1)}, u32[]{:S(2)}, u32[]{:S(2)}) async-start(f32[64,1,128]{2,1,0:T(1,128)} %bitcast.8), calls=%async_computation.1 | async-start | bytes 65536 | tf_op jit(solution)/shard_map/all_to_all | solution.py:600
  67.1 0.0 collective-permute-done.3.came_above.above
  67.1 0.0 copy-start.1
  67.1 0.0 collective-permute-done.4.came_below.below
  67.2 0.0 copy-start.2
  67.2 0.6 copy-done.1
  67.8 0.0 copy-done.2
  67.8 27.2 %near.1 = f32[2,16,32,128]{3,2,1,0:T(8,128)} custom-call(s32[2]{0:T(128)} %pad_add_fusion.place, f32[3,16,32,128]{3,2,1,0:T(8,128)} %settle.1.own, f32[3,16,32,128]{3,2,1,0:T(8,128)} %copy-done, f32[2,16,32,128]{3,2,1,0:T(8,128)} %inner.1.after, f32[112,128]{1,0:T(8,128)} %get-tuple-element.20.from_left, f32[112,128]{1,0:T(8,128)} %get-tuple-element.21.from_right, ...), custom_call_target="tpu_custom_call" | custom-call | tf_op jit(solution)/shard_map/near/pallas_call | solution.py:617
  95.0 0.0 all-to-all-done.1
  95.0 0.6 copy-done.3
  95.6 9.1 %far.1 = f32[2,16,32,128]{3,2,1,0:T(8,128)} custom-call(s32[2]{0:T(128)} %pad_add_fusion.place, f32[3,16,32,128]{3,2,1,0:T(8,128)} %settle.1.own, f32[2,16,32,128]{3,2,1,0:T(8,128)} %near.1, f32[2480,128]{1,0:T(8,128)} %get-tuple-element.15.after.cells, f32[112,128]{1,0:T(8,128)} %get-tuple-element.20.from_left, f32[112,128]{1,0:T(8,128)} %get-tuple-element.21.from_right, ...), custom_call_target="tpu_custom_call" | custom-call | tf_op jit(solution)/shard_map/far/pallas_call | solution.py:650
  (2 shorter events, 0.0 us)
Async XLA Ops:
  30.3 6.4 %collective-permute-start = (f32[3,16,32,128]{3,2,1,0:T(8,128)}, f32[3,16,32,128]{3,2,1,0:T(8,128)S(1)}, u32[]{:S(2)}, u32[]{:S(2)}) collective-permute-start(f32[3,16,32,128]{3,2,1,0:T(8,128)} %settle.1.own), channel_id=1, source_target_pairs={{0,1},{1,0},{2,3},{3,2},{4,5},{5,4},{6,7},{7,6},{8,9},{9,8},{10,11... | collective-permute-start | bytes 2359304 | tf_op jit(solution)/shard_map/ppermute | solution.py:578
  36.7 0.9 copy-start
  43.8 12.9 %collective-permute-start.1 = (f32[112,128]{1,0:T(8,128)}, f32[112,128]{1,0:T(8,128)S(1)}, u32[]{:S(2)}, u32[]{:S(2)}) collective-permute-start(f32[112,128]{1,0:T(8,128)} %get-tuple-element.18), channel_id=1, source_target_pairs={{0,8},{8,16},{16,24},{24,32},{32,40},{40,48},{48,56},{56,64},{64,7... | collective-permute-start | bytes 172040 | tf_op jit(solution)/shard_map/ppermute | solution.py:571
  44.4 12.3 %collective-permute-start.2 = (f32[112,128]{1,0:T(8,128)}, f32[112,128]{1,0:T(8,128)S(1)}, u32[]{:S(2)}, u32[]{:S(2)}) collective-permute-start(f32[112,128]{1,0:T(8,128)} %get-tuple-element.19), channel_id=1, source_target_pairs={{0,120},{8,0},{16,8},{24,16},{32,24},{40,32},{48,40},{56,48},{64,5... | collective-permute-start | bytes 172040 | tf_op jit(solution)/shard_map/ppermute | solution.py:571
  56.7 0.6 copy-start.4
  56.7 0.6 copy-start.5
  59.3 7.9 %collective-permute-start.3 = (f32[264,128]{1,0:T(8,128)}, f32[264,128]{1,0:T(8,128)S(1)}, u32[]{:S(2)}, u32[]{:S(2)}) collective-permute-start(f32[264,128]{1,0:T(8,128)} %get-tuple-element.22), channel_id=1, source_target_pairs={{0,2},{2,4},{4,6},{6,0},{1,3},{3,5},{5,7},{7,1},{8,10},{10,12},{12... | collective-permute-start | bytes 405512 | tf_op jit(solution)/shard_map/ppermute | solution.py:571
  60.8 6.3 %collective-permute-start.4 = (f32[264,128]{1,0:T(8,128)}, f32[264,128]{1,0:T(8,128)S(1)}, u32[]{:S(2)}, u32[]{:S(2)}) collective-permute-start(f32[264,128]{1,0:T(8,128)} %get-tuple-element.23), channel_id=1, source_target_pairs={{0,6},{2,0},{4,2},{6,4},{1,7},{3,1},{5,3},{7,5},{8,14},{10,8},{12,... | collective-permute-start | bytes 405512 | tf_op jit(solution)/shard_map/ppermute | solution.py:571
  62.5 32.5 %all-to-all-start.1 = ((f32[64,1,128]{2,1,0:T(1,128)}), f32[64,1,128]{2,1,0:T(1,128)S(1)}, u32[]{:S(2)}, u32[]{:S(2)}) async-start(f32[64,1,128]{2,1,0:T(1,128)} %bitcast.8), calls=%async_computation.1 | async-start | bytes 65536 | tf_op jit(solution)/shard_map/all_to_all | solution.py:600
  67.1 0.6 copy-start.1
  67.2 0.7 copy-start.2
  95.0 0.6 copy-start.3

commit v5 on v4

--- a/solution.py
+++ b/solution.py
@@ -206,7 +206,7 @@
             return sums
 
         sums = lax.fori_loop(
-            0, 16, add_slot, tuple(jnp.zeros((8, LANES), f32) for _ in range(CHAN)), unroll=2
+            0, 16, add_slot, tuple(jnp.zeros((8, LANES), f32) for _ in range(CHAN)), unroll=4
         )
         for c in range(CHAN):
             mom[pl.ds(8 * tile * CHAN + c, 8, stride=CHAN), :] = sums[c]
@@ -355,7 +355,7 @@
                     return sources[0, j, rows, :], y + float(dy) if dy else y, sources[2, j, rows, :]
 
                 steps.append(source)
-            acc = add_sources(acc, own, tile, group, steps, 16, 4)
+            acc = add_sources(acc, own, tile, group, steps, 16, 8)
             store_group(out, acc, tile, group)
 
 
@@ -388,7 +388,11 @@
                         before = before - 1.0
                         after = after + 1.0
                     src[0, m, place, :] = before
-                    src[1, m, place, :] = middle
+                    if part == 0:
+                        src[1, m, pl.ds(8, 8), :] = middle[0:8]
+                        src[1, m, pl.ds(32, 8), :] = middle[24:32]
+                    else:
+                        src[1, m, place, :] = middle
                     src[2, m, place, :] = after
 
     for tile in range(4):
@@ -409,7 +413,7 @@
                         return src[dx, j, rows, :], y + float(dy) if dy else y, src[dx, 64 + j, rows, :]
 
                     steps.append(source)
-            acc = add_sources(acc, own, tile, group, steps, 32, 2)
+            acc = add_sources(acc, own, tile, group, steps, 32, 4)
             store_group(out, acc, tile, group)
 
 
@@ -555,7 +559,7 @@
             out[1, j, rows, :] = (re + near[0, j, rows, :]) * scale
             return 0
 
-        lax.fori_loop(0, 16, value, 0, unroll=2)
+        lax.fori_loop(0, 16, value, 0, unroll=4)
 
 
 def params():

time: 106 us -> 105 us (level)
  transfers between devices with their start and end apart: 6 -> 6, of which waited for: 0 -> 0; matrix products, arithmetic and copies ran while one was open for 1% -> 1% of each run, Pallas kernels for 39% -> 38%
where the time goes in v5:
time: 105 us; the launch traced here: 104 us
  Pallas kernels  70.2 us (67%)
  blocking collectives  16.8 us (16%)
  starting transfers between devices  13.4 us (13%)
  local copies, waits for them, and re-layouts  2.8 us (3%)
    pallas_call x1, Pallas kernels, fields(): pl.pallas_call(near_kernel, in_specs=[smem] + [vmem] * 7, out_shape=shape...  26.7 us
    all_to_all x1, blocking collectives, local(): arrived = lax.all_to_all(outgoing, 'cell', 0, 0, tiled=True)  16.8 us
    pallas_call x1, Pallas kernels, fields(): pl.pallas_call(far_kernel, grid_spec=pltpu.PrefetchScalarGridSpec(num_sca...  8.93 us
    ppermute x4, starting transfers between devices, neighbours(): lax.ppermute(value, axis, [(i, (i + step) % size) for i in range(size)])  8.58 us
    pallas_call x1, Pallas kernels, local(): pl.pallas_call(settle_kernel, out_shape=shape(3, 16, 32, LANES), scratch_...  7.29 us
    pallas_call x1, Pallas kernels, fields(): pl.pallas_call(functools.partial(inner_kernel, add=True), in_specs=[vmem]...  6.73 us
    pallas_call x1, Pallas kernels, fields(): pl.pallas_call(lambda own, out: inner_kernel(own, own, None, None, out, a...  6.29 us
    pallas_call x1, Pallas kernels, local(): pl.pallas_call(pack_kernel, out_shape=shape(16, 4, 8, LANES), scratch_sha...  6.27 us
  transfers between devices with their start and end apart: 6, of which 0 were waited for; matrix products, arithmetic and copies ran while one was open for 1% of the time, Pallas kernels for 38%

profile of v5, /device:TPU:0, one launch (start us, length us, event | category | flops | bytes accessed | tf_op | source)
XLA Modules:
  0.0 103.9 jit_solution(125614391537918885)
XLA Ops:
  0.0 6.3 %pack.1 = f32[16,4,8,128]{3,2,1,0:T(8,128)} custom-call(f32[2,32,128]{2,1,0:T(8,128)} %bitcast.12, f32[32,128]{1,0:T(8,128)} %bitcast.13, s32[32,128]{1,0:T(8,128)} %bitcast.14, s32[32,128]{1,0:T(8,128)} %bitcast.15, s32[32,128]{1,0:T(8,128)} %bitcast.16), custom_call_target="tpu_custom_call" | custom-call | tf_op jit(solution)/shard_map/pack/pallas_call | solution.py:822
  6.3 16.8 %all_to_all.16.arrived = f32[16,4,8,128]{3,2,1,0:T(8,128)} all-to-all(f32[16,4,8,128]{3,2,1,0:T(8,128)} %pack.1), channel_id=1, replica_groups=mesh['cell'=16,'level'=4,'rep'=2] {'cell'}, dimensions={0} | all-to-all | bytes 524288 | tf_op jit(solution)/shard_map/all_to_all | solution.py:835
  23.0 7.3 %settle.1.own = f32[3,16,32,128]{3,2,1,0:T(8,128)} custom-call(f32[16,4,8,128]{3,2,1,0:T(8,128)} %all_to_all.16.arrived, f32[2,16,32,128]{3,2,1,0:T(8,128)} %pos.1, f32[16,32,128]{2,1,0:T(8,128)} %strength.1), custom_call_target="tpu_custom_call" | custom-call | tf_op jit(solution)/shard_map/settle/pallas_call | solution.py:836
  30.3 0.0 collective-permute-start
  30.3 6.3 %inner_own.1.after.earlier = f32[2,16,32,128]{3,2,1,0:T(8,128)} custom-call(f32[3,16,32,128]{3,2,1,0:T(8,128)} %settle.1.own), custom_call_target="tpu_custom_call" | custom-call | tf_op jit(solution)/shard_map/inner_own/pallas_call | solution.py:583
  36.6 0.0 collective-permute-done.other.sources
  36.6 0.0 copy-start
  36.6 0.9 copy-done
  37.5 6.1 %upward.1 = (f32[2480,128]{1,0:T(8,128)}, f32[112,128]{1,0:T(8,128)}, f32[112,128]{1,0:T(8,128)}, f32[264,128]{1,0:T(8,128)}, f32[264,128]{1,0:T(8,128)}, /*index=5*/f32[64,128]{1,0:T(8,128)}) custom-call(f32[2,16,32,128]{3,2,1,0:T(8,128)} %inner_own.1.after.earlier, f32[3,16,32,128]{3,2,1,0:T(8,128)} %settle.1.own, f32[3,16,32,128]{3,2,1,0:T(8,128)} %copy-done, ...), custom_call_target="tpu_custom_call" | custom-call | tf_op jit(solution)/shard_map/upward/pallas_call | solution.py:594
  43.6 0.6 collective-permute-start.1
  44.2 4.8 %collective-permute-start.2 = (f32[112,128]{1,0:T(8,128)}, f32[112,128]{1,0:T(8,128)S(1)}, u32[]{:S(2)}, u32[]{:S(2)}) collective-permute-start(f32[112,128]{1,0:T(8,128)} %get-tuple-element.19), channel_id=1, source_target_pairs={{0,120},{8,0},{16,8},{24,16},{32,24},{40,32},{48,40},{56,48},{64,5... | collective-permute-start | bytes 172040 | tf_op jit(solution)/shard_map/ppermute | solution.py:575
  48.9 0.6 pad_add_fusion.place
  49.6 6.7 %inner.1.after = f32[2,16,32,128]{3,2,1,0:T(8,128)} custom-call(f32[3,16,32,128]{3,2,1,0:T(8,128)} %settle.1.own, f32[3,16,32,128]{3,2,1,0:T(8,128)} %copy-done, f32[2,16,32,128]{3,2,1,0:T(8,128)} %inner_own.1.after.earlier, f32[2480,128]{1,0:T(8,128)} %get-tuple-element.15.after.cells), custom_call_target="tpu_custom_call" | custom-call | tf_op jit(solution)/shard_map/inner/pallas_call | solution.py:605
  56.3 0.0 collective-permute-done.1.came_left
  56.3 0.0 collective-permute-done.2.came_right
  56.3 0.0 copy-start.5
  56.3 0.6 copy-done.4
  56.9 0.0 copy-done.5
  57.0 1.9 %rows.1 = (f32[264,128]{1,0:T(8,128)}, f32[264,128]{1,0:T(8,128)}, f32[112,128]{1,0:T(8,128)}, f32[112,128]{1,0:T(8,128)}) custom-call(s32[2]{0:T(128)} %pad_add_fusion.place, f32[2,16,32,128]{3,2,1,0:T(8,128)} %inner.1.after, f32[264,128]{1,0:T(8,128)} %get-tuple-element.16.top, f32[264,128]{1,0:T(8,128)} %get-tuple-element.17.bottom, ...), custom_call_target="tpu_custom_call" | custom-call | tf_op jit(solution)/shard_map/rows/pallas_call | solution.py:612
  58.9 1.6 %collective-permute-start.3 = (f32[264,128]{1,0:T(8,128)}, f32[264,128]{1,0:T(8,128)S(1)}, u32[]{:S(2)}, u32[]{:S(2)}) collective-permute-start(f32[264,128]{1,0:T(8,128)} %get-tuple-element.22), channel_id=1, source_target_pairs={{0,2},{2,4},{4,6},{6,0},{1,3},{3,5},{5,7},{7,1},{8,10},{10,12},{12... | collective-permute-start | bytes 405512 | tf_op jit(solution)/shard_map/ppermute | solution.py:575
  60.5 1.7 %collective-permute-start.4 = (f32[264,128]{1,0:T(8,128)}, f32[264,128]{1,0:T(8,128)S(1)}, u32[]{:S(2)}, u32[]{:S(2)}) collective-permute-start(f32[264,128]{1,0:T(8,128)} %get-tuple-element.23), channel_id=1, source_target_pairs={{0,6},{2,0},{4,2},{6,4},{1,7},{3,1},{5,3},{7,5},{8,14},{10,8},{12,... | collective-permute-start | bytes 405512 | tf_op jit(solution)/shard_map/ppermute | solution.py:575
  62.1 4.8 %all-to-all-start.1 = ((f32[64,1,128]{2,1,0:T(1,128)}), f32[64,1,128]{2,1,0:T(1,128)S(1)}, u32[]{:S(2)}, u32[]{:S(2)}) async-start(f32[64,1,128]{2,1,0:T(1,128)} %bitcast.8), calls=%async_computation.1 | async-start | bytes 65536 | tf_op jit(solution)/shard_map/all_to_all | solution.py:604
  67.0 0.0 collective-permute-done.3.came_above.above
  67.0 0.0 copy-start.1
  67.0 0.0 collective-permute-done.4.came_below.below
  67.0 0.0 copy-start.2
  67.0 0.6 copy-done.1
  67.6 0.0 copy-done.2
  67.7 26.7 %near.1 = f32[2,16,32,128]{3,2,1,0:T(8,128)} custom-call(s32[2]{0:T(128)} %pad_add_fusion.place, f32[3,16,32,128]{3,2,1,0:T(8,128)} %settle.1.own, f32[3,16,32,128]{3,2,1,0:T(8,128)} %copy-done, f32[2,16,32,128]{3,2,1,0:T(8,128)} %inner.1.after, f32[112,128]{1,0:T(8,128)} %get-tuple-element.20.from_left, f32[112,128]{1,0:T(8,128)} %get-tuple-element.21.from_right, ...), custom_call_target="tpu_custom_call" | custom-call | tf_op jit(solution)/shard_map/near/pallas_call | solution.py:621
  94.4 0.0 all-to-all-done.1
  94.4 0.6 copy-done.3
  95.0 8.9 %far.1 = f32[2,16,32,128]{3,2,1,0:T(8,128)} custom-call(s32[2]{0:T(128)} %pad_add_fusion.place, f32[3,16,32,128]{3,2,1,0:T(8,128)} %settle.1.own, f32[2,16,32,128]{3,2,1,0:T(8,128)} %near.1, f32[2480,128]{1,0:T(8,128)} %get-tuple-element.15.after.cells, f32[112,128]{1,0:T(8,128)} %get-tuple-element.20.from_left, f32[112,128]{1,0:T(8,128)} %get-tuple-element.21.from_right, ...), custom_call_target="tpu_custom_call" | custom-call | tf_op jit(solution)/shard_map/far/pallas_call | solution.py:654
  (2 shorter events, 0.0 us)
Async XLA Ops:
  30.3 6.3 %collective-permute-start = (f32[3,16,32,128]{3,2,1,0:T(8,128)}, f32[3,16,32,128]{3,2,1,0:T(8,128)S(1)}, u32[]{:S(2)}, u32[]{:S(2)}) collective-permute-start(f32[3,16,32,128]{3,2,1,0:T(8,128)} %settle.1.own), channel_id=1, source_target_pairs={{0,1},{1,0},{2,3},{3,2},{4,5},{5,4},{6,7},{7,6},{8,9},{9,8},{10,11... | collective-permute-start | bytes 2359304 | tf_op jit(solution)/shard_map/ppermute | solution.py:582
  36.6 0.9 copy-start
  43.6 12.7 %collective-permute-start.1 = (f32[112,128]{1,0:T(8,128)}, f32[112,128]{1,0:T(8,128)S(1)}, u32[]{:S(2)}, u32[]{:S(2)}) collective-permute-start(f32[112,128]{1,0:T(8,128)} %get-tuple-element.18), channel_id=1, source_target_pairs={{0,8},{8,16},{16,24},{24,32},{32,40},{40,48},{48,56},{56,64},{64,7... | collective-permute-start | bytes 172040 | tf_op jit(solution)/shard_map/ppermute | solution.py:575
  44.2 12.2 %collective-permute-start.2 = (f32[112,128]{1,0:T(8,128)}, f32[112,128]{1,0:T(8,128)S(1)}, u32[]{:S(2)}, u32[]{:S(2)}) collective-permute-start(f32[112,128]{1,0:T(8,128)} %get-tuple-element.19), channel_id=1, source_target_pairs={{0,120},{8,0},{16,8},{24,16},{32,24},{40,32},{48,40},{56,48},{64,5... | collective-permute-start | bytes 172040 | tf_op jit(solution)/shard_map/ppermute | solution.py:575
  56.3 0.6 copy-start.4
  56.3 0.6 copy-start.5
  58.9 8.1 %collective-permute-start.3 = (f32[264,128]{1,0:T(8,128)}, f32[264,128]{1,0:T(8,128)S(1)}, u32[]{:S(2)}, u32[]{:S(2)}) collective-permute-start(f32[264,128]{1,0:T(8,128)} %get-tuple-element.22), channel_id=1, source_target_pairs={{0,2},{2,4},{4,6},{6,0},{1,3},{3,5},{5,7},{7,1},{8,10},{10,12},{12... | collective-permute-start | bytes 405512 | tf_op jit(solution)/shard_map/ppermute | solution.py:575
  60.5 6.5 %collective-permute-start.4 = (f32[264,128]{1,0:T(8,128)}, f32[264,128]{1,0:T(8,128)S(1)}, u32[]{:S(2)}, u32[]{:S(2)}) collective-permute-start(f32[264,128]{1,0:T(8,128)} %get-tuple-element.23), channel_id=1, source_target_pairs={{0,6},{2,0},{4,2},{6,4},{1,7},{3,1},{5,3},{7,5},{8,14},{10,8},{12,... | collective-permute-start | bytes 405512 | tf_op jit(solution)/shard_map/ppermute | solution.py:575
  62.1 32.3 %all-to-all-start.1 = ((f32[64,1,128]{2,1,0:T(1,128)}), f32[64,1,128]{2,1,0:T(1,128)S(1)}, u32[]{:S(2)}, u32[]{:S(2)}) async-start(f32[64,1,128]{2,1,0:T(1,128)} %bitcast.8), calls=%async_computation.1 | async-start | bytes 65536 | tf_op jit(solution)/shard_map/all_to_all | solution.py:604
  67.0 0.6 copy-start.1
  67.0 0.7 copy-start.2
  94.4 0.6 copy-start.3
